TPU v7x, 512 devices: a whole 4x8x8 slice. The times are simulated.
512 devices in a mesh: batch: 4 (over z_lo), rows: 16 (over y, core), cols: 8 (over z_hi, x).
Axes of the slice: x: 4, y: 8, z: 8 (z_hi: 2, z_lo: 4; z = z_hi * 4 + z_lo), core: 2. Of those that a mesh axis runs over, the one named last changes fastest.
Arguments:
- features: bfloat16 [1024, 512, 1024], P(('batch', 'rows'), 'cols'), parts along dimension 0, may hold values from -6 to 6
- qkv_weight: bfloat16 [1024, 1536], replicated, may hold values from -10 to 10
- orders: int32 [64, 32, 256], P(('batch', 'rows'), 'cols'), parts along dimension 0, may hold values from 0 to 255, each once within a row
Outputs:
- attended: bfloat16 [1024, 512, 512], P(('batch', 'rows'), 'cols'), parts along dimension 0
There are 4 independent parts, one for each index of `batch`. A program takes and returns all parts, laid end to end along the dimension named above; an argument that names none is the same for every part. Nothing has to cross between parts.
All inputs are finite; a program needn't handle non-finite values.
Results may differ from a plain program's by a relative error of at most 0.0078.
Values may be sent and summed in bfloat16 or wider, within the bound.
No kernel may reach another device: no remote copies, remote signals or barrier semaphores. Data moves between devices by JAX's collectives and lax.ppermute only.
A program may use at most 128 MiB of HBM per device.

v0:
```python
import jax
import jax.numpy as jnp
from jax import lax
from jax.sharding import PartitionSpec as P

HEADS = 8
HEAD_DIM = 64
WINDOW = 16
HALF_WINDOW = 8
TOKEN_WIN = 256
INNER_DIM = 512


EPSILON = 1e-06


def passed_along(shard, axis, by):
    size = lax.axis_size(axis)
    return lax.ppermute(shard, axis, [(i, (i + by) % size) for i in range(size)])


def window_labels(first_row, first_col, win_down, win_across, total_rows, total_cols):
    row_index = (first_row + jnp.arange(win_down, dtype=jnp.int32)) % total_rows
    col_index = (first_col + jnp.arange(win_across, dtype=jnp.int32)) % total_cols
    row_last = row_index == total_rows - 1
    col_last = col_index == total_cols - 1
    position = jnp.arange(TOKEN_WIN, dtype=jnp.int32)
    lower_half = position // WINDOW >= HALF_WINDOW
    right_half = position % WINDOW >= HALF_WINDOW
    row_label = (row_last[:, None, None] & lower_half[None, None, :]).astype(jnp.int32)
    col_label = (col_last[None, :, None] & right_half[None, None, :]).astype(jnp.int32)
    return (2 * row_label + col_label).reshape(win_down * win_across, TOKEN_WIN)


def attend(block_in, qkv_weight, orders, first_row, first_col, total_rows, total_cols):
    height, breadth, channels = block_in.shape
    win_down = height // WINDOW
    win_across = breadth // WINDOW
    count = win_down * win_across
    blocks = block_in.reshape(win_down, WINDOW, win_across, WINDOW, channels)
    blocks = blocks.transpose(0, 2, 1, 3, 4).reshape(count * TOKEN_WIN, channels)
    widened = blocks.astype(jnp.float32)
    center = jnp.mean(widened, axis=-1, keepdims=True)
    spread = jnp.mean(jnp.square(widened - center), axis=-1, keepdims=True)
    normed = ((widened - center) * lax.rsqrt(spread + EPSILON)).astype(jnp.bfloat16)
    packed = jnp.dot(normed, qkv_weight, preferred_element_type=jnp.float32).astype(jnp.bfloat16)
    packed = packed.reshape(count, TOKEN_WIN, 3, HEADS, HEAD_DIM)
    query_heads = packed[:, :, 0]
    key_heads = packed[:, :, 1]
    value_heads = packed[:, :, 2]
    scores = jnp.einsum(
        "wqhd,wkhd->whqk", query_heads, key_heads, preferred_element_type=jnp.float32
    )
    scores = scores * HEAD_DIM ** (-0.5)
    labels = window_labels(first_row, first_col, win_down, win_across, total_rows, total_cols)
    ranks = orders.reshape(count, TOKEN_WIN)
    allowed = (ranks[:, None, :] <= ranks[:, :, None]) & (labels[:, None, :] == labels[:, :, None])
    masked = jnp.where(allowed[:, None], scores, -jnp.inf)
    row_max = jnp.max(masked, axis=-1, keepdims=True)
    lifted = jnp.exp(masked - row_max)
    weights = (lifted / jnp.sum(lifted, axis=-1, keepdims=True)).astype(jnp.bfloat16)
    mixed = jnp.einsum("whqk,wkhd->wqhd", weights, value_heads, preferred_element_type=jnp.float32)
    mixed = mixed.astype(jnp.bfloat16).reshape(win_down, win_across, WINDOW, WINDOW, INNER_DIM)
    return mixed.transpose(0, 2, 1, 3, 4).reshape(height, breadth, INNER_DIM)


def per_device(features, qkv_weight, orders):
    height, breadth, channels = features.shape
    row_device = lax.axis_index("rows")
    col_device = lax.axis_index("cols")
    win_down = height // WINDOW
    win_across = breadth // WINDOW
    total_rows = lax.axis_size("rows") * win_down
    total_cols = lax.axis_size("cols") * win_across
    upper = passed_along(features[:HALF_WINDOW], "rows", -1)
    tall = jnp.concatenate([features[HALF_WINDOW:], upper], axis=0)
    beside = passed_along(tall[:, :HALF_WINDOW], "cols", -1)
    framed = jnp.concatenate([tall[:, HALF_WINDOW:], beside], axis=1)
    local_out = attend(
        framed,
        qkv_weight,
        orders,
        row_device * win_down,
        col_device * win_across,
        total_rows,
        total_cols,
    )
    lower = passed_along(local_out[height - HALF_WINDOW :], "rows", 1)
    settled = jnp.concatenate([lower, local_out[: height - HALF_WINDOW]], axis=0)
    trailing = passed_along(settled[:, breadth - HALF_WINDOW :], "cols", 1)
    return jnp.concatenate([trailing, settled[:, : breadth - HALF_WINDOW]], axis=1)


def solution(mesh):
    in_specs = (P(("batch", "rows"), "cols", None), P(), P(("batch", "rows"), "cols", None))
    out_specs = P(("batch", "rows"), "cols", None)
    return jax.shard_map(
        per_device, mesh=mesh, in_specs=in_specs, out_specs=out_specs, check_vma=False
    )
```

profile of v0, /device:TPU:64, one launch (start us, length us, event | category | flops | bytes accessed | tf_op | source)
XLA Modules:
  0.0 122.8 jit_solution(16689216351355901072)
XLA Ops:
  0.0 3.3 %fusion.27 = (bf16[8,64,1024]{2,1,0:T(8,128)(2,1)}, bf16[8,64,1024]{2,1,0:T(8,128)(2,1)}) fusion(bf16[16,64,1024]{2,1,0:T(8,128)(2,1)} %param.3), kind=kLoop, calls=%fused_computation.53 | loop fusion | bytes 4194304 | tf_op jit(solution)/shard_map/slice | solution.py:76
  3.3 2.9 %collective-permute-start = (bf16[8,64,1024]{2,1,0:T(8,128)(2,1)}, bf16[8,64,1024]{2,1,0:T(8,128)(2,1)}, u32[]{:S(2)}, u32[]{:S(2)}) collective-permute-start(bf16[8,64,1024]{2,1,0:T(8,128)(2,1)} %get-tuple-element.9), channel_id=1, source_target_pairs={{0,120},{8,0},{16,8},{24,16},{32,24},{40,32},{48,40},{56,48},{64,5... | collective-permute-start | bytes 3145736 | tf_op jit(solution)/shard_map/ppermute | solution.py:19
  6.3 12.5 %collective-permute-done = bf16[8,64,1024]{2,1,0:T(8,128)(2,1)} collective-permute-done((bf16[8,64,1024]{2,1,0:T(8,128)(2,1)}, bf16[8,64,1024]{2,1,0:T(8,128)(2,1)}, u32[]{:S(2)}, u32[]{:S(2)}) %collective-permute-start) | collective-permute-done | bytes 1048608 | tf_op jit(solution)/shard_map/ppermute | solution.py:19
  19.8 12.2 %collective-permute-start.1 = (bf16[16,8,1024]{2,1,0:T(8,128)(2,1)S(1)}, bf16[16,8,1024]{2,1,0:T(8,128)(2,1)S(1)}, u32[]{:S(2)}, u32[]{:S(2)}) collective-permute-start(bf16[16,8,1024]{2,1,0:T(8,128)(2,1)S(1)} %pad_maximum_fusion.2), channel_id=1, source_target_pairs={{0,7},{1,0},{2,1},{3,2},{4,3},{5,4},{6,5},{7,6},{8,15},{9,8},{10,9... | collective-permute-start | bytes 786440 | tf_op jit(solution)/shard_map/ppermute | solution.py:19
  32.4 1.6 %fusion.9 = bf16[16,56,1024]{2,1,0:T(8,128)(2,1)S(1)} fusion(bf16[8,64,1024]{2,1,0:T(8,128)(2,1)} %get-tuple-element.8, bf16[8,64,1024]{2,1,0:T(8,128)(2,1)} %collective-permute-done), kind=kLoop, calls=%fused_computation.19 | loop fusion | flops 917504 | bytes 3932160 | tf_op jit(solution)/shard_map/concatenate | solution.py:76
  34.0 8.3 %collective-permute-done.1 = bf16[16,8,1024]{2,1,0:T(8,128)(2,1)S(1)} collective-permute-done((bf16[16,8,1024]{2,1,0:T(8,128)(2,1)S(1)}, bf16[16,8,1024]{2,1,0:T(8,128)(2,1)S(1)}, u32[]{:S(2)}, u32[]{:S(2)}) %collective-permute-start.1) | collective-permute-done | bytes 262176 | tf_op jit(solution)/shard_map/ppermute | solution.py:19
  42.5 1.3 %copy-done.2 = bf16[16,64,1024]{2,1,0:T(8,128)(2,1)} copy-done((bf16[16,64,1024]{2,1,0:T(8,128)(2,1)}, bf16[16,64,1024]{2,1,0:T(8,128)(2,1)S(1)}, u32[]{:S(2)}) %copy-start.2) | copy-done | bytes 2097176
  44.3 4.2 %convert_bitcast_fusion = f32[1,4,16,16,1024]{4,3,1,2,0:T(8,128)} fusion(bf16[1,16,4,16,1024]{4,3,2,1,0:T(8,128)(2,1)} %bitcast.36), kind=kLoop, calls=%fused_computation.5 | loop fusion | flops 1048576 | bytes 6291456 | tf_op jit(solution)/shard_map/convert_element_type | solution.py:42
  49.3 2.8 %copy.37 = f32[1,4,16,16,1024]{4,3,2,1,0:T(8,128)S(1)} copy(f32[1,4,16,16,1024]{4,3,1,2,0:T(8,128)} %convert_bitcast_fusion) | data formatting | bytes 8388608 | tf_op jit(solution)/shard_map/convert_element_type | solution.py:42
  52.5 4.9 %convolution_convert_fusion = bf16[1024,1536]{1,0:T(8,128)(2,1)} fusion(bf16[1024,1024]{1,0:T(8,128)(2,1)S(1)} %fusion.3, bf16[1024,1536]{1,0:T(8,128)(2,1)S(1)} %copy-done), kind=kOutput, calls=%fused_computation.14 | convolution fusion | flops 3222798336 | bytes 8388608 | tf_op jit(solution)/shard_map/dot_general | solution.py:46
  57.4 8.9 %reshape.202 = bf16[4,256,3,8,64]{4,3,2,1,0:T(8,128)(2,1)} reshape(bf16[1024,1536]{1,0:T(8,128)(2,1)} %convolution_convert_fusion) | data formatting | bytes 6291456 | tf_op jit(solution)/shard_map/reshape | solution.py:47
  66.2 5.3 %fusion.26 = (bf16[4,256,1,8,64]{4,3,2,1,0:T(8,128)(2,1)}, bf16[4,256,1,8,64]{4,3,2,1,0:T(8,128)(2,1)}, bf16[4,256,1,8,64]{4,3,2,1,0:T(8,128)(2,1)S(1)}) fusion(bf16[4,256,3,8,64]{4,3,2,1,0:T(8,128)(2,1)} %reshape.202), kind=kLoop, calls=%fused_computation.52 | loop fusion | bytes 6291456 | tf_op jit(solution)/shard_map/slice | solution.py:50
  71.5 3.0 %copy.52 = bf16[4,256,1,8,64]{1,4,3,0,2:T(8,128)(2,1)} copy(bf16[4,256,1,8,64]{4,3,2,1,0:T(8,128)(2,1)} %get-tuple-element.5) | data formatting | bytes 2097152
  74.5 2.2 %copy.53 = bf16[4,256,1,8,64]{1,4,3,0,2:T(8,128)(2,1)S(1)} copy(bf16[4,256,1,8,64]{4,3,2,1,0:T(8,128)(2,1)} %get-tuple-element.6) | data formatting | bytes 2097152
  76.8 1.9 %copy.54 = bf16[4,256,1,8,64]{1,4,3,0,2:T(8,128)(2,1)} copy(bf16[4,256,1,8,64]{4,3,2,1,0:T(8,128)(2,1)S(1)} %get-tuple-element.7) | data formatting | bytes 2097152
  78.7 2.5 %fusion.13 = f32[4,8,256,256]{2,3,1,0:T(8,128)S(1)} fusion(bf16[4,256,1,8,64]{1,4,3,0,2:T(8,128)(2,1)} %copy.54, bf16[4,256,1,8,64]{1,4,3,0,2:T(8,128)(2,1)S(1)} %copy.53), kind=kOutput, calls=%fused_computation.24 | convolution fusion | flops 268435456 | bytes 10485760 | tf_op jit(solution)/shard_map/wqhd,wkhd->whqk/dot_general | solution.py:51
  81.2 4.5 %fusion.29 = (f32[4,8,256]{2,1,0:T(8,128)S(1)}, f32[4,8,256,256]{2,3,1,0:T(8,128)}) fusion(f32[4,8,256,256]{2,3,1,0:T(8,128)S(1)} %fusion.13, pred[4,256,256]{1,2,0:T(8,128)(4,1)S(1)} %compare_and_fusion), kind=kOutput, calls=%fused_computation.55 | output fusion | flops 12583167 | bytes 17072128 | tf_op jit(solution)/shard_map/sub | solution.py:60
  85.7 4.2 %fusion.11 = bf16[4,256,8,64]{1,3,2,0:T(8,128)(2,1)S(1)} fusion(f32[4,8,256,256]{2,3,1,0:T(8,128)} %get-tuple-element.13, f32[4,8,256]{2,1,0:T(8,128)S(1)} %get-tuple-element.12, bf16[4,256,1,8,64]{1,4,3,0,2:T(8,128)(2,1)S(1)} %copy-done.4), kind=kOutput, calls=%fused_computation.21 | convolution fusion | flops 273154048 | bytes 10518528 | tf_op jit(solution)/shard_map/whqk,wkhd->wqhd/dot_general | solution.py:62
  90.0 2.1 %copy.46 = bf16[4,256,8,64]{3,2,1,0:T(8,128)(2,1)} copy(bf16[4,256,8,64]{1,3,2,0:T(8,128)(2,1)S(1)} %fusion.11) | data formatting | bytes 2097152 | tf_op jit(solution)/shard_map/convert_element_type | solution.py:63
  92.1 4.2 %reshape.198 = bf16[1,4,16,16,512]{4,3,2,1,0:T(8,128)(2,1)} reshape(bf16[4,256,8,64]{3,2,1,0:T(8,128)(2,1)} %copy.46) | data formatting | bytes 2097152 | tf_op jit(solution)/shard_map/reshape | solution.py:63
  96.3 1.3 %fusion.28 = (bf16[1,8,4,16,512]{4,3,1,2,0:T(8,128)(2,1)S(1)}, bf16[1,8,4,16,512]{4,3,1,2,0:T(8,128)(2,1)S(1)}) fusion(bf16[1,16,4,16,512]{4,3,1,2,0:T(8,128)(2,1)} %bitcast.40), kind=kLoop, calls=%fused_computation.54 | loop fusion | bytes 2097152 | tf_op jit(solution)/shard_map/slice | solution.py:88
  97.7 9.9 %collective-permute-done.2 = bf16[8,64,512]{2,1,0:T(8,128)(2,1)S(1)} collective-permute-done((bf16[8,64,512]{2,1,0:T(8,128)(2,1)S(1)}, bf16[8,64,512]{2,1,0:T(8,128)(2,1)S(1)}, u32[]{:S(2)}, u32[]{:S(2)}) %collective-permute-start.2) | collective-permute-done | bytes 524320 | tf_op jit(solution)/shard_map/ppermute | solution.py:19
  107.6 1.9 %collective-permute-start.3 = (bf16[16,8,512]{2,1,0:T(8,128)(2,1)S(1)}, bf16[16,8,512]{2,1,0:T(8,128)(2,1)S(1)}, u32[]{:S(2)}, u32[]{:S(2)}) collective-permute-start(bf16[16,8,512]{2,1,0:T(8,128)(2,1)S(1)} %pad_maximum_fusion.3), channel_id=1, source_target_pairs={{0,1},{1,2},{2,3},{3,4},{4,5},{5,6},{6,7},{7,0},{8,9},{9,10},{10,1... | collective-permute-start | bytes 393224 | tf_op jit(solution)/shard_map/ppermute | solution.py:19
  109.6 12.2 %collective-permute-done.3 = bf16[16,8,512]{2,1,0:T(8,128)(2,1)S(1)} collective-permute-done((bf16[16,8,512]{2,1,0:T(8,128)(2,1)S(1)}, bf16[16,8,512]{2,1,0:T(8,128)(2,1)S(1)}, u32[]{:S(2)}, u32[]{:S(2)}) %collective-permute-start.3) | collective-permute-done | bytes 131104 | tf_op jit(solution)/shard_map/ppermute | solution.py:19
  (31 shorter events, 4.5 us)
Async XLA Ops:
  0.0 52.5 %copy-start = (bf16[1024,1536]{1,0:T(8,128)(2,1)S(1)}, bf16[1024,1536]{1,0:T(8,128)(2,1)}, u32[]{:S(2)}) copy-start(bf16[1024,1536]{1,0:T(8,128)(2,1)} %param.4) | copy-start | bytes 9437188
  0.0 32.0 %copy-start.5 = (s32[1,4,256]{2,1,0:T(4,128)S(1)}, s32[1,4,256]{2,1,0:T(4,128)}, u32[]{:S(2)}) copy-start(s32[1,4,256]{2,1,0:T(4,128)} %param.5) | copy-start | bytes 12292
  3.3 15.5 %collective-permute-start = (bf16[8,64,1024]{2,1,0:T(8,128)(2,1)}, bf16[8,64,1024]{2,1,0:T(8,128)(2,1)}, u32[]{:S(2)}, u32[]{:S(2)}) collective-permute-start(bf16[8,64,1024]{2,1,0:T(8,128)(2,1)} %get-tuple-element.9), channel_id=1, source_target_pairs={{0,120},{8,0},{16,8},{24,16},{32,24},{40,32},{48,40},{56,48},{64,5... | collective-permute-start | bytes 3145736 | tf_op jit(solution)/shard_map/ppermute | solution.py:19
  19.8 22.5 %collective-permute-start.1 = (bf16[16,8,1024]{2,1,0:T(8,128)(2,1)S(1)}, bf16[16,8,1024]{2,1,0:T(8,128)(2,1)S(1)}, u32[]{:S(2)}, u32[]{:S(2)}) collective-permute-start(bf16[16,8,1024]{2,1,0:T(8,128)(2,1)S(1)} %pad_maximum_fusion.2), channel_id=1, source_target_pairs={{0,7},{1,0},{2,1},{3,2},{4,3},{5,4},{6,5},{7,6},{8,15},{9,8},{10,9... | collective-permute-start | bytes 786440 | tf_op jit(solution)/shard_map/ppermute | solution.py:19
  42.5 1.3 %copy-start.2 = (bf16[16,64,1024]{2,1,0:T(8,128)(2,1)}, bf16[16,64,1024]{2,1,0:T(8,128)(2,1)S(1)}, u32[]{:S(2)}) copy-start(bf16[16,64,1024]{2,1,0:T(8,128)(2,1)S(1)} %pad_maximum_fusion) | copy-start | bytes 6291460
  44.3 4.2 %copy-start.3 = (bf16[16,64,1024]{2,1,0:T(8,128)(2,1)S(1)}, bf16[16,64,1024]{2,1,0:T(8,128)(2,1)}, u32[]{:S(2)}) copy-start(bf16[16,64,1024]{2,1,0:T(8,128)(2,1)} %copy-done.2) | copy-start | bytes 6291460
  81.2 4.5 %copy-start.4 = (bf16[4,256,1,8,64]{1,4,3,0,2:T(8,128)(2,1)S(1)}, bf16[4,256,1,8,64]{1,4,3,0,2:T(8,128)(2,1)}, u32[]{:S(2)}) copy-start(bf16[4,256,1,8,64]{1,4,3,0,2:T(8,128)(2,1)} %copy.52) | copy-start | bytes 3145732
  92.1 30.7 %copy-start.1 = (bf16[1024,1536]{1,0:T(8,128)(2,1)S(1)}, bf16[1024,1536]{1,0:T(8,128)(2,1)}, u32[]{:S(2)}) copy-start(bf16[1024,1536]{1,0:T(8,128)(2,1)} %param.4) | copy-start | bytes 9437188
  97.7 10.0 %collective-permute-start.2 = (bf16[8,64,512]{2,1,0:T(8,128)(2,1)S(1)}, bf16[8,64,512]{2,1,0:T(8,128)(2,1)S(1)}, u32[]{:S(2)}, u32[]{:S(2)}) collective-permute-start(bf16[8,64,512]{2,1,0:T(8,128)(2,1)S(1)} %bitcast.41), channel_id=1, source_target_pairs={{0,8},{8,16},{16,24},{24,32},{32,40},{40,48},{48,56},{56,64},{64,7... | collective-permute-start | bytes 1572872 | tf_op jit(solution)/shard_map/ppermute | solution.py:19
  107.6 14.2 %collective-permute-start.3 = (bf16[16,8,512]{2,1,0:T(8,128)(2,1)S(1)}, bf16[16,8,512]{2,1,0:T(8,128)(2,1)S(1)}, u32[]{:S(2)}, u32[]{:S(2)}) collective-permute-start(bf16[16,8,512]{2,1,0:T(8,128)(2,1)S(1)} %pad_maximum_fusion.3), channel_id=1, source_target_pairs={{0,1},{1,2},{2,3},{3,4},{4,5},{5,6},{6,7},{7,0},{8,9},{9,10},{10,1... | collective-permute-start | bytes 393224 | tf_op jit(solution)/shard_map/ppermute | solution.py:19
where the time goes:
time: 123 us
  waiting for transfers between devices  43 us (35%)
  local copies, waits for them, and re-layouts  36.5 us (30%)
  starting transfers between devices  17.1 us (14%)
  other arithmetic  14.5 us (12%)
  matrix products  11.6 us (9%)
    ppermute x4, waiting for transfers between devices, passed_along(): lax.ppermute(shard, axis, [(i, (i + by) % size) for i in range(size)])  43 us
    ppermute x4, starting transfers between devices, passed_along(): lax.ppermute(shard, axis, [(i, (i + by) % size) for i in range(size)])  17.1 us
    reshape x1, local copies, waits for them, and re-layouts, attend(): packed = packed.reshape(count, TOKEN_WIN, 3, HEADS, HEAD_DIM)  8.86 us
    unnamed x15, local copies, waits for them, and re-layouts  8.49 us
    slice x1, local copies, waits for them, and re-layouts, attend(): value_heads = packed[:, :, 2]  5.28 us
    dot_general x1, matrix products, attend(): jnp.dot(normed, qkv_weight, preferred_element_type=jnp.float32)  4.89 us
    sub x1, other arithmetic, attend(): lifted = jnp.exp(masked - row_max)  4.51 us
    dot_general x1, matrix products, attend(): jnp.einsum('whqk,wkhd->wqhd', weights, value_heads, preferred_element_typ...  4.23 us
  transfers between devices with their start and end apart: 4, of which 4 were waited for; matrix products, arithmetic and copies ran while one was open for 2% of the time, Pallas kernels for 0%

commit v1 on v0

v1 whole, which is shorter than its diff:
```python
import jax
import jax.numpy as jnp
from jax import lax
from jax.experimental import pallas as pl
from jax.experimental.pallas import tpu as pltpu
from jax.sharding import PartitionSpec as P

D = 1024
HEADS = 8
HEAD_DIM = 64
INNER = 512
HALF = 8
EPSILON = 1e-06
LOG2E = 1.4426950408889634
FAR = 4096.0
BF = jnp.bfloat16
F32 = jnp.float32
MIB = 1 << 20


def normalize(values):
    center = jnp.mean(values, axis=-1, keepdims=True)
    off = values - center
    spread = jnp.mean(off * off, axis=-1, keepdims=True)
    return off * lax.rsqrt(spread + EPSILON)


def pack_kernel(x_ref, ord_ref, up_a, up_b, dn_a, dn_b, e1, e2):
    odd = lax.rem(lax.axis_index("cols"), 2) == 1
    for h, (a_ref, b_ref) in enumerate(((up_a, up_b), (dn_a, dn_b))):

        def two_rows(t, _, h=h, a_ref=a_ref, b_ref=b_ref):
            rows = [x_ref[h * HALF + 2 * t + u].astype(F32) for u in range(2)]
            for j in range(3):
                for u in range(2):
                    part = normalize(rows[u][8 + 16 * j : 24 + 16 * j]).astype(BF)
                    ref, base = (a_ref, 128 * j) if j < 2 else (b_ref, 0)
                    ref[pl.ds(pl.multiple_of(base + (2 * t + u) * 16, 16), 16), :] = part
            left = normalize(jnp.concatenate([rows[0][:8], rows[1][:8]], axis=0)).astype(BF)
            right = normalize(jnp.concatenate([rows[0][56:], rows[1][56:]], axis=0)).astype(BF)
            b_ref[pl.ds(pl.multiple_of(128 + t * 16, 16), 16), :] = left
            b_ref[pl.ds(pl.multiple_of(192 + t * 16, 16), 16), :] = right
            at = pl.ds(pl.multiple_of(64 * h + t * 16, 16), 16)
            e1[at, :] = jnp.where(odd, right, left)
            e2[at, :] = jnp.where(odd, left, right)
            return 0

        lax.fori_loop(0, 4, two_rows, 0)
    ranks = ord_ref[0].astype(F32).astype(BF)
    natural = lax.broadcasted_iota(jnp.int32, (256, 256), 0)
    m = lax.broadcasted_iota(jnp.int32, (256, 256), 1)
    source = ((m >> 7) * 8 + ((m >> 3) & 7)) * 16 + ((m >> 6) & 1) * 8 + (m & 7)
    quads = jnp.dot(ranks, (natural == source).astype(F32).astype(BF), preferred_element_type=F32)
    rank_row = jnp.concatenate(
        [ranks[0:1].astype(F32), ranks[1:2].astype(F32), ranks[2:3].astype(F32), quads[3:4]], axis=1
    )
    block = jnp.broadcast_to(rank_row, (16, D)).astype(BF)
    dn_a[256:272, :] = block
    e1[128:144, :] = block
    e2[128:144, :] = block


def project_kernel(ua, ub, da, db, w_ref, pa, pb):
    for h, (a_ref, b_ref) in enumerate(((ua, ub), (da, db))):
        for src, dst in ((a_ref, pa), (b_ref, pb)):
            dst[h] = jnp.dot(src[0:256, :], w_ref[...], preferred_element_type=F32).astype(BF)


def column_of(row, count):
    q = lax.broadcasted_iota(jnp.int32, (count, 128), 0)
    lane = lax.broadcasted_iota(jnp.int32, (count, 128), 1)
    return jnp.sum(jnp.where(q == lane, jnp.broadcast_to(row, (count, 128)), 0.0), axis=1, keepdims=True)


def attend(query, keys, values, allowed):
    count = query.shape[0]
    both = jnp.concatenate([allowed, allowed], axis=0)
    first = lax.broadcasted_iota(jnp.int32, (count, 128), 1) < HEAD_DIM
    ones = jnp.ones((256, 128), BF)
    outs = []
    for g in range(4):
        at = slice(128 * g, 128 * g + 128)
        q = query[:, at]
        zero = jnp.zeros_like(q)
        q = jnp.concatenate([jnp.where(first, q, zero), jnp.where(first, zero, q)], axis=0)
        s = lax.dot_general(q, keys[:, at], (((1,), (1,)), ((), ())), preferred_element_type=F32)
        s = jnp.where(both, s, -jnp.inf)
        top = jnp.max(s, axis=-1, keepdims=True)
        p = jnp.exp2((s - top) * (LOG2E * HEAD_DIM**-0.5)).astype(BF)
        o = jnp.dot(p, jnp.concatenate([values[:, at], ones], axis=1), preferred_element_type=F32)
        number = jnp.where(first, o[:count, :128], o[count:, :128])
        total = jnp.where(first, o[:count, 128:], o[count:, 128:])
        outs.append(number / total)
    return jnp.concatenate(outs, axis=1)


def inner_window(h, j, own, other_kv, rank_row, last, out):
    own_ranks = rank_row[:, 128:] if h == 0 else rank_row[:, :128]
    other_ranks = (rank_row[:, :128] if h == 0 else rank_row[:, 128:]) + jnp.where(last, FAR, 0.0)
    key_ranks = jnp.concatenate([own_ranks, other_ranks], axis=1)
    allowed = key_ranks <= column_of(own_ranks, 128)
    keys = jnp.concatenate([own[:, INNER : 2 * INNER], other_kv[:, :INNER]], axis=0)
    values = jnp.concatenate([own[:, 2 * INNER :], other_kv[:, INNER:]], axis=0)
    out[h, j] = attend(own[:, :INNER], keys, values, allowed).astype(BF)


def last_pair(h):
    size = lax.axis_size("rows")
    return lax.axis_index("rows") == (0 if h == 0 else size - 1)


def inner_a_kernel(up_a, dn_a, pa, w_ref, ord_ref, oa):
    for h, src in enumerate((dn_a, up_a)):
        kv = jnp.dot(src[0:256, :], w_ref[:, INNER:], preferred_element_type=F32).astype(BF)
        for j in range(2):
            if h == 0:
                ranks = dn_a[256:272, 256 * j : 256 * j + 256].astype(F32)[0:1]
            else:
                ranks = ord_ref[0, j : j + 1, :].astype(F32)
            at = slice(128 * j, 128 * j + 128)
            inner_window(h, j, pa[h, at, :], kv[at], ranks, last_pair(h), oa)


def inner_b_kernel(up_b, dn_b, dn_a, pb, w_ref, ord_ref, ob, kve):
    for h, src in enumerate((dn_b, up_b)):
        kv = jnp.dot(src[0:256, :], w_ref[:, INNER:], preferred_element_type=F32).astype(BF)
        if h == 0:
            ranks = dn_a[256:272, 512:768].astype(F32)[0:1]
        else:
            ranks = ord_ref[0, 2:3, :].astype(F32)
        inner_window(h, 0, pb[h, 0:128, :], kv[0:128], ranks, last_pair(h), ob)
        kve[h, 0] = kv[128:192]
        kve[h, 1] = kv[192:256]


def strips_kernel(e1, e2, w_ref, kvf):
    for e, src in enumerate((e1, e2)):
        kv = jnp.dot(src[0:128, :], w_ref[:, INNER:], preferred_element_type=F32).astype(BF)
        kvf[e, 0] = kv[0:64]
        kvf[e, 1] = kv[64:128]


def edge_kernel(hop_u, hop_d, e1, e2, dn_a, pb, kve, kvf, oa, ob, w_ref, ord_ref, out, edge):
    col = lax.axis_index("cols")
    odd = lax.rem(col, 2)
    natural = lax.broadcasted_iota(jnp.int32, (256, 256), 0)
    m = lax.broadcasted_iota(jnp.int32, (256, 256), 1)
    source = ((m >> 7) * 8 + ((m >> 3) & 7)) * 16 + ((m >> 6) & 1) * 8 + (m & 7)
    own_ranks = ord_ref[0].astype(F32).astype(BF)
    mine = jnp.dot(own_ranks, (natural == source).astype(F32).astype(BF), preferred_element_type=F32)[3:4]
    above = dn_a[256:272, 768:1024].astype(F32)[0:1]
    diag = jnp.concatenate([hop_d[0:64, :], hop_d[80:144, :], hop_u[0:128, :]], axis=0)
    kvd = jnp.dot(diag, w_ref[:, INNER:], preferred_element_type=F32).astype(BF)
    for e, strip in enumerate((e1, e2)):
        side = odd if e == 0 else 1 - odd
        is_left = side == 0
        beside = strip[128:144, 768:1024].astype(F32)[0:1]
        corner = hop_d[80 * e + 64 : 80 * e + 80, 768:1024].astype(F32)[0:1]
        last_col = jnp.where(is_left, col == 0, col == lax.axis_size("cols") - 1)
        for h in range(2):
            ranks = jnp.where(is_left, corner, above) if h == 0 else jnp.where(is_left, beside, mine)
            half_own = ranks[:, 128:] if h == 0 else ranks[:, :128]
            half_other = ranks[:, :128] if h == 0 else ranks[:, 128:]
            half_own = jnp.where(is_left, jnp.concatenate([half_own[:, 64:], half_own[:, :64]], axis=1), half_own)
            half_other = jnp.where(is_left, jnp.concatenate([half_other[:, 64:], half_other[:, :64]], axis=1), half_other)
            lane = lax.broadcasted_iota(jnp.int32, (1, 128), 1)
            far_col = jnp.where((lane >= 64) & last_col, FAR, 0.0)
            key_ranks = jnp.concatenate(
                [half_own + far_col, half_other + far_col + jnp.where(last_pair(h), FAR, 0.0)], axis=1
            )
            allowed = key_ranks <= column_of(half_own, 64)
            own = pb[h, pl.ds(pl.multiple_of(128 + 64 * side, 64), 64), :]
            near = kve[h, side]
            far = kvf[e, h]
            cross = kvd[128 * h + 64 * e : 128 * h + 64 * e + 64]
            keys = jnp.concatenate([own[:, INNER : 2 * INNER], far[:, :INNER], near[:, :INNER], cross[:, :INNER]], axis=0)
            values = jnp.concatenate([own[:, 2 * INNER :], far[:, INNER:], near[:, INNER:], cross[:, INNER:]], axis=0)
            edge[h, side] = attend(own[:, :INNER], keys, values, allowed)
    for h in range(2):
        for i in range(HALF):
            row = jnp.concatenate(
                [
                    edge[h, 0, 8 * i : 8 * i + 8],
                    oa[h, 0, 16 * i : 16 * i + 16].astype(F32),
                    oa[h, 1, 16 * i : 16 * i + 16].astype(F32),
                    ob[h, 0, 16 * i : 16 * i + 16].astype(F32),
                    edge[h, 1, 8 * i : 8 * i + 8],
                ],
                axis=0,
            )
            out[h * HALF + i] = row.astype(BF)


def call(kernel, outs, args, flops, scratch=(), limit=40):
    sizes = sum(a.size * a.dtype.itemsize for a in args) + sum(o.size * o.dtype.itemsize for o in outs)
    single = len(outs) == 1
    vmem = pl.BlockSpec(memory_space=pltpu.VMEM)
    return pl.pallas_call(
        kernel,
        out_shape=outs[0] if single else tuple(outs),
        in_specs=[vmem] * len(args),
        out_specs=vmem if single else tuple([vmem] * len(outs)),
        scratch_shapes=list(scratch),
        compiler_params=pltpu.CompilerParams(vmem_limit_bytes=limit * MIB),
        cost_estimate=pl.CostEstimate(flops=flops, bytes_accessed=sizes, transcendentals=0),
    )(*args)


def arr(*shape):
    return jax.ShapeDtypeStruct(shape, BF)


def along_rows(value, by):
    size = lax.axis_size("rows")
    return lax.ppermute(value, "rows", [(i, (i + by) % size) for i in range(size)])


def per_device(features, qkv_weight, orders):
    cols = lax.axis_size("cols")
    up_a, up_b, dn_a, dn_b, e1, e2 = call(
        pack_kernel,
        [arr(256, D), arr(256, D), arr(272, D), arr(256, D), arr(144, D), arr(144, D)],
        [features, orders],
        20_000_000,
    )
    first = [(c, (c + 1) % cols if c % 2 else (c - 1) % cols) for c in range(cols)]
    second = [(c, (c - 1) % cols if c % 2 else (c + 1) % cols) for c in range(cols)]
    got_e1 = lax.ppermute(e1, "cols", first)
    got_up_a = along_rows(up_a, -1)
    got_dn_a = along_rows(dn_a, 1)
    got_up_b = along_rows(up_b, -1)
    got_dn_b = along_rows(dn_b, 1)
    got_e2 = lax.ppermute(e2, "cols", second)
    pa, pb = call(
        project_kernel, [arr(2, 256, 3 * INNER)] * 2, [up_a, up_b, dn_a, dn_b, qkv_weight], 3_200_000_000
    )
    oa = call(
        inner_a_kernel, [arr(2, 2, 128, INNER)], [got_up_a, got_dn_a, pa, qkv_weight, orders], 4_000_000_000
    )
    ob, kve = call(
        inner_b_kernel,
        [arr(2, 1, 128, INNER), arr(2, 2, 64, 2 * INNER)],
        [got_up_b, got_dn_b, got_dn_a, pb, qkv_weight, orders],
        3_000_000_000,
    )
    hop_u = along_rows(jnp.concatenate([got_e1[0:64], got_e2[0:64]], axis=0), -1)
    hop_d = along_rows(jnp.concatenate([got_e1[64:144], got_e2[64:144]], axis=0), 1)
    kvf = call(strips_kernel, [arr(2, 2, 64, 2 * INNER)], [got_e1, got_e2, qkv_weight], 600_000_000)
    return call(
        edge_kernel,
        [arr(16, 64, INNER)],
        [hop_u, hop_d, got_e1, got_e2, got_dn_a, pb, kve, kvf, oa, ob, qkv_weight, orders],
        2_000_000_000,
        scratch=[pltpu.VMEM((2, 2, 64, INNER), F32)],
    )


def solution(mesh):
    in_specs = (P(("batch", "rows"), "cols", None), P(), P(("batch", "rows"), "cols", None))
    out_specs = P(("batch", "rows"), "cols", None)
    return jax.shard_map(
        per_device, mesh=mesh, in_specs=in_specs, out_specs=out_specs, check_vma=False
    )
```

time: 123 us -> 50 us (0.41)
  the two profiles are of different devices: /device:TPU:64 before, /device:TPU:96 now
where the time goes in v1:
time: 50 us; the launch traced here: 49.8 us
  starting transfers between devices  20.1 us (40%)
  Pallas kernels  13.7 us (27%)
  waiting for transfers between devices  11.6 us (23%)
  local copies, waits for them, and re-layouts  4.22 us (8%)
    pallas_call x6, Pallas kernels, call(): pl.pallas_call(kernel, out_shape=outs[0] if single else tuple(outs), in_s...  13.7 us
    ppermute x1, starting transfers between devices, per_device(): got_e1 = lax.ppermute(e1, 'cols', first)  12.2 us
    ppermute x1, waiting for transfers between devices, per_device(): got_e1 = lax.ppermute(e1, 'cols', first)  6.87 us
    ppermute x6, starting transfers between devices, along_rows(): lax.ppermute(value, 'rows', [(i, (i + by) % size) for i in range(size)])  5.99 us
    ppermute x6, waiting for transfers between devices, along_rows(): lax.ppermute(value, 'rows', [(i, (i + by) % size) for i in range(size)])  4.72 us
    unnamed x10, local copies, waits for them, and re-layouts  4.17 us
    ppermute x1, starting transfers between devices, per_device(): got_e2 = lax.ppermute(e2, 'cols', second)  1.92 us
  transfers between devices with their start and end apart: 8, of which 3 were waited for; matrix products, arithmetic and copies ran while one was open for 0% of the time, Pallas kernels for 18%

profile of v1, /device:TPU:96, one launch (start us, length us, event | category | flops | bytes accessed | tf_op | source)
XLA Modules:
  0.0 49.8 jit_solution(6574758841135424297)
XLA Ops:
  0.0 1.6 %copy-done.2 = bf16[16,64,1024]{2,1,0:T(8,128)(2,1)S(1)} copy-done((bf16[16,64,1024]{2,1,0:T(8,128)(2,1)S(1)}, bf16[16,64,1024]{2,1,0:T(8,128)(2,1)}, u32[]{:S(2)}) %copy-start.2) | copy-done | bytes 2097176
  1.6 0.7 %copy-done.3 = s32[1,4,256]{2,1,0:T(4,128)S(1)} copy-done((s32[1,4,256]{2,1,0:T(4,128)S(1)}, s32[1,4,256]{2,1,0:T(4,128)}, u32[]{:S(2)}) %copy-start.3) | copy-done | bytes 4120
  2.3 2.1 %shard_map.37 = (bf16[256,1024]{1,0:T(8,128)(2,1)S(1)}, bf16[256,1024]{1,0:T(8,128)(2,1)S(1)}, bf16[272,1024]{1,0:T(8,128)(2,1)S(1)}, bf16[256,1024]{1,0:T(8,128...) custom-call(bf16[16,64,1024]{2,1,0:T(8,128)(2,1)S(1)} %copy-done.2, s32[1,4,256]{2,1,0:T(4,128)S(1)} %copy-done.3), custom_call_target="tpu_custom_call" | custom-call | flops 20000000 | bytes 4820992 | tf_op jit(solution)/shard_map/pallas_call | solution.py:198
  4.4 3.0 %collective-permute-start.5 = (bf16[256,1024]{1,0:T(8,128)(2,1)S(1)}, bf16[256,1024]{1,0:T(8,128)(2,1)S(1)}, u32[]{:S(2)}, u32[]{:S(2)}) collective-permute-start(bf16[256,1024]{1,0:T(8,128)(2,1)S(1)} %get-tuple-element.19.ub), channel_id=1, source_target_pairs={{0,120},{8,0},{16,8},{24,16},{32,24},{40,32},{48,40},{56,48},{64,5... | collective-permute-start | bytes 1572872 | tf_op jit(solution)/shard_map/ppermute | solution.py:215
  7.4 0.0 collective-permute-start.7
  7.4 12.2 %collective-permute-start = (bf16[144,1024]{1,0:T(8,128)(2,1)S(1)}, bf16[144,1024]{1,0:T(8,128)(2,1)S(1)}, u32[]{:S(2)}, u32[]{:S(2)}) collective-permute-start(bf16[144,1024]{1,0:T(8,128)(2,1)S(1)} %get-tuple-element.15), channel_id=1, source_target_pairs={{0,7},{1,2},{2,1},{3,4},{4,3},{5,6},{6,5},{7,0},{8,15},{9,10},{10,... | collective-permute-start | bytes 884744 | tf_op jit(solution)/shard_map/ppermute | solution.py:228
  19.6 1.9 %collective-permute-start.1 = (bf16[144,1024]{1,0:T(8,128)(2,1)S(1)}, bf16[144,1024]{1,0:T(8,128)(2,1)S(1)}, u32[]{:S(2)}, u32[]{:S(2)}) collective-permute-start(bf16[144,1024]{1,0:T(8,128)(2,1)S(1)} %get-tuple-element.16), channel_id=1, source_target_pairs={{0,1},{1,0},{2,3},{3,2},{4,5},{5,4},{6,7},{7,6},{8,9},{9,8},{10,11... | collective-permute-start | bytes 884744 | tf_op jit(solution)/shard_map/ppermute | solution.py:233
  21.6 0.0 copy-start
  21.6 1.9 %copy-done = bf16[1024,1536]{1,0:T(8,128)(2,1)S(1)} copy-done((bf16[1024,1536]{1,0:T(8,128)(2,1)S(1)}, bf16[1024,1536]{1,0:T(8,128)(2,1)}, u32[]{:S(2)}) %copy-start) | copy-done | bytes 3145752
  23.5 3.4 %shard_map.38 = (bf16[2,256,1536]{2,1,0:T(8,128)(2,1)S(1)}, bf16[2,256,1536]{2,1,0:T(8,128)(2,1)S(1)}) custom-call(bf16[256,1024]{1,0:T(8,128)(2,1)S(1)} %get-tuple-element.18.ua, bf16[256,1024]{1,0:T(8,128)(2,1)S(1)} %get-tuple-element.19.ub, bf16[272,1024]{1,0:T(8,128)(2,1)S(1)} %get-tuple-element.17.da, bf16[256,1024]{1,0:T(8,128)(2,1)S(1)} %get-tuple-element.20.db, ...), custom_call_target="tpu_custom_call" | custom-call | flops 3200000000 | bytes 8421376 | tf_op jit(solution)/shard_map/pallas_call | solution.py:198
  26.9 6.9 %collective-permute-done.e1 = bf16[144,1024]{1,0:T(8,128)(2,1)S(1)} collective-permute-done((bf16[144,1024]{1,0:T(8,128)(2,1)S(1)}, bf16[144,1024]{1,0:T(8,128)(2,1)S(1)}, u32[]{:S(2)}, u32[]{:S(2)}) %collective-permute-start) | collective-permute-done | bytes 294944 | tf_op jit(solution)/shard_map/ppermute | solution.py:228
  33.7 0.0 collective-permute-start.6
  33.8 0.0 collective-permute-done.1.e2
  33.8 0.0 collective-permute-start.3
  33.9 0.0 copy-start.4
  33.9 0.7 %shard_map.40.kvf = bf16[2,2,64,1024]{3,2,1,0:T(8,128)(2,1)S(1)} custom-call(bf16[144,1024]{1,0:T(8,128)(2,1)S(1)} %collective-permute-done.e1, bf16[144,1024]{1,0:T(8,128)(2,1)S(1)} %collective-permute-done.1.e2, bf16[1024,1536]{1,0:T(8,128)(2,1)S(1)} %copy-done.1), custom_call_target="tpu_custom_call" | custom-call | flops 600000000 | bytes 4259840 | tf_op jit(solution)/shard_map/pallas_call | solution.py:198
  34.7 3.0 %collective-permute-start.2 = (bf16[128,1024]{1,0:T(8,128)(2,1)S(1)}, bf16[128,1024]{1,0:T(8,128)(2,1)S(1)}, u32[]{:S(2)}, u32[]{:S(2)}) collective-permute-start(bf16[128,1024]{1,0:T(8,128)(2,1)S(1)} %pad_maximum_fusion.1), channel_id=1, source_target_pairs={{0,120},{8,0},{16,8},{24,16},{32,24},{40,32},{48,40},{56,48},{64,5... | collective-permute-start | bytes 786440 | tf_op jit(solution)/shard_map/ppermute | solution.py:215
  37.6 0.0 collective-permute-done.4.dn_a
  37.6 2.7 %shard_map.41.oa = bf16[2,2,128,512]{3,2,1,0:T(8,128)(2,1)S(1)} custom-call(bf16[256,1024]{1,0:T(8,128)(2,1)S(1)} %collective-permute-done.7.up_a, bf16[272,1024]{1,0:T(8,128)(2,1)S(1)} %collective-permute-done.4.dn_a, bf16[2,256,1536]{2,1,0:T(8,128)(2,1)S(1)} %get-tuple-element.23.pa, bf16[1024,1536]{1,0:T(8,128)(2,1)S(1)} %copy-done.1, ...), custom_call_target="tpu_custom_call" | custom-call | flops 4000000000 | bytes 6328320 | tf_op jit(solution)/shard_map/pallas_call | solution.py:198
  40.3 0.0 collective-permute-done.5.up_b
  40.3 3.2 %collective-permute-done.6.dn_b = bf16[256,1024]{1,0:T(8,128)(2,1)S(1)} collective-permute-done((bf16[256,1024]{1,0:T(8,128)(2,1)S(1)}, bf16[256,1024]{1,0:T(8,128)(2,1)S(1)}, u32[]{:S(2)}, u32[]{:S(2)}) %collective-permute-start.6) | collective-permute-done | bytes 524320 | tf_op jit(solution)/shard_map/ppermute | solution.py:215
  43.6 2.0 %shard_map.39 = (bf16[2,1,128,512]{3,2,1,0:T(8,128)(2,1)S(1)}, bf16[2,2,64,1024]{3,2,1,0:T(8,128)(2,1)S(1)}) custom-call(bf16[256,1024]{1,0:T(8,128)(2,1)S(1)} %collective-permute-done.5.up_b, bf16[256,1024]{1,0:T(8,128)(2,1)S(1)} %collective-permute-done.6.dn_b, bf16[272,1024]{1,0:T(8,128)(2,1)S(1)} %collective-permute-done.4.dn_a, ...), custom_call_target="tpu_custom_call" | custom-call | flops 3000000000 | bytes 7114752 | tf_op jit(solution)/shard_map/pallas_call | solution.py:198
  45.6 1.5 %collective-permute-done.3.hop_d = bf16[160,1024]{1,0:T(8,128)(2,1)S(1)} collective-permute-done((bf16[160,1024]{1,0:T(8,128)(2,1)S(1)}, bf16[160,1024]{1,0:T(8,128)(2,1)S(1)}, u32[]{:S(2)}, u32[]{:S(2)}) %collective-permute-start.3) | collective-permute-done | bytes 327712 | tf_op jit(solution)/shard_map/ppermute | solution.py:215
  47.1 2.7 %shard_map.42 = bf16[16,64,512]{2,1,0:T(8,128)(2,1)} custom-call(bf16[128,1024]{1,0:T(8,128)(2,1)S(1)} %collective-permute-done.2.hop_u, bf16[160,1024]{1,0:T(8,128)(2,1)S(1)} %collective-permute-done.3.hop_d, bf16[144,1024]{1,0:T(8,128)(2,1)S(1)} %collective-permute-done.e1, bf16[144,1024]{1,0:T(8,128)(2,1)S(1)} %collective-permute-done.1.e2, ...), custom_call_target="tpu_custom_call" | custom-call | flops 2000000000 | bytes 9342976 | tf_op jit(solution)/shard_map/pallas_call | solution.py:198
  (14 shorter events, 0.1 us)
Async XLA Ops:
  0.0 1.6 %copy-start.2 = (bf16[16,64,1024]{2,1,0:T(8,128)(2,1)S(1)}, bf16[16,64,1024]{2,1,0:T(8,128)(2,1)}, u32[]{:S(2)}) copy-start(bf16[16,64,1024]{2,1,0:T(8,128)(2,1)} %x_ref.1) | copy-start | bytes 6291460
  1.6 0.7 %copy-start.3 = (s32[1,4,256]{2,1,0:T(4,128)S(1)}, s32[1,4,256]{2,1,0:T(4,128)}, u32[]{:S(2)}) copy-start(s32[1,4,256]{2,1,0:T(4,128)} %ord_ref.7) | copy-start | bytes 12292
  4.4 33.2 %collective-permute-start.4 = (bf16[272,1024]{1,0:T(8,128)(2,1)S(1)}, bf16[272,1024]{1,0:T(8,128)(2,1)S(1)}, u32[]{:S(2)}, u32[]{:S(2)}) collective-permute-start(bf16[272,1024]{1,0:T(8,128)(2,1)S(1)} %get-tuple-element.17.da), channel_id=1, source_target_pairs={{0,8},{8,16},{16,24},{24,32},{32,40},{40,48},{48,56},{56,64},{64,7... | collective-permute-start | bytes 1671176 | tf_op jit(solution)/shard_map/ppermute | solution.py:215
  4.4 35.9 %collective-permute-start.5 = (bf16[256,1024]{1,0:T(8,128)(2,1)S(1)}, bf16[256,1024]{1,0:T(8,128)(2,1)S(1)}, u32[]{:S(2)}, u32[]{:S(2)}) collective-permute-start(bf16[256,1024]{1,0:T(8,128)(2,1)S(1)} %get-tuple-element.19.ub), channel_id=1, source_target_pairs={{0,120},{8,0},{16,8},{24,16},{32,24},{40,32},{48,40},{56,48},{64,5... | collective-permute-start | bytes 1572872 | tf_op jit(solution)/shard_map/ppermute | solution.py:215
  7.4 27.3 %collective-permute-start.7 = (bf16[256,1024]{1,0:T(8,128)(2,1)S(1)}, bf16[256,1024]{1,0:T(8,128)(2,1)S(1)}, u32[]{:S(2)}, u32[]{:S(2)}) collective-permute-start(bf16[256,1024]{1,0:T(8,128)(2,1)S(1)} %get-tuple-element.18.ua), channel_id=1, source_target_pairs={{0,120},{8,0},{16,8},{24,16},{32,24},{40,32},{48,40},{56,48},{64,5... | collective-permute-start | bytes 1572872 | tf_op jit(solution)/shard_map/ppermute | solution.py:215
  7.4 26.3 %collective-permute-start = (bf16[144,1024]{1,0:T(8,128)(2,1)S(1)}, bf16[144,1024]{1,0:T(8,128)(2,1)S(1)}, u32[]{:S(2)}, u32[]{:S(2)}) collective-permute-start(bf16[144,1024]{1,0:T(8,128)(2,1)S(1)} %get-tuple-element.15), channel_id=1, source_target_pairs={{0,7},{1,2},{2,1},{3,4},{4,3},{5,6},{6,5},{7,0},{8,15},{9,10},{10,... | collective-permute-start | bytes 884744 | tf_op jit(solution)/shard_map/ppermute | solution.py:228
  19.6 14.1 %collective-permute-start.1 = (bf16[144,1024]{1,0:T(8,128)(2,1)S(1)}, bf16[144,1024]{1,0:T(8,128)(2,1)S(1)}, u32[]{:S(2)}, u32[]{:S(2)}) collective-permute-start(bf16[144,1024]{1,0:T(8,128)(2,1)S(1)} %get-tuple-element.16), channel_id=1, source_target_pairs={{0,1},{1,0},{2,3},{3,2},{4,5},{5,4},{6,7},{7,6},{8,9},{9,8},{10,11... | collective-permute-start | bytes 884744 | tf_op jit(solution)/shard_map/ppermute | solution.py:233
  21.6 1.9 %copy-start = (bf16[1024,1536]{1,0:T(8,128)(2,1)S(1)}, bf16[1024,1536]{1,0:T(8,128)(2,1)}, u32[]{:S(2)}) copy-start(bf16[1024,1536]{1,0:T(8,128)(2,1)} %w_ref.9) | copy-start | bytes 9437188
  23.4 10.4 %copy-start.1 = (bf16[1024,1536]{1,0:T(8,128)(2,1)S(1)}, bf16[1024,1536]{1,0:T(8,128)(2,1)}, u32[]{:S(2)}) copy-start(bf16[1024,1536]{1,0:T(8,128)(2,1)} %w_ref.9) | copy-start | bytes 9437188
  33.7 9.8 %collective-permute-start.6 = (bf16[256,1024]{1,0:T(8,128)(2,1)S(1)}, bf16[256,1024]{1,0:T(8,128)(2,1)S(1)}, u32[]{:S(2)}, u32[]{:S(2)}) collective-permute-start(bf16[256,1024]{1,0:T(8,128)(2,1)S(1)} %get-tuple-element.20.db), channel_id=1, source_target_pairs={{0,8},{8,16},{16,24},{24,32},{32,40},{40,48},{48,56},{56,64},{64,7... | collective-permute-start | bytes 1572872 | tf_op jit(solution)/shard_map/ppermute | solution.py:215
  33.8 13.2 %collective-permute-start.3 = (bf16[160,1024]{1,0:T(8,128)(2,1)S(1)}, bf16[160,1024]{1,0:T(8,128)(2,1)S(1)}, u32[]{:S(2)}, u32[]{:S(2)}) collective-permute-start(bf16[160,1024]{1,0:T(8,128)(2,1)S(1)} %pad_maximum_fusion), channel_id=1, source_target_pairs={{0,8},{8,16},{16,24},{24,32},{32,40},{40,48},{48,56},{56,64},{64,7... | collective-permute-start | bytes 983048 | tf_op jit(solution)/shard_map/ppermute | solution.py:215
  33.9 3.7 %copy-start.4 = (s32[1,4,256]{2,1,0:T(4,128)S(1)}, s32[1,4,256]{2,1,0:T(4,128)}, u32[]{:S(2)}) copy-start(s32[1,4,256]{2,1,0:T(4,128)} %ord_ref.7) | copy-start | bytes 12292
  34.7 10.9 %collective-permute-start.2 = (bf16[128,1024]{1,0:T(8,128)(2,1)S(1)}, bf16[128,1024]{1,0:T(8,128)(2,1)S(1)}, u32[]{:S(2)}, u32[]{:S(2)}) collective-permute-start(bf16[128,1024]{1,0:T(8,128)(2,1)S(1)} %pad_maximum_fusion.1), channel_id=1, source_target_pairs={{0,120},{8,0},{16,8},{24,16},{32,24},{40,32},{48,40},{56,48},{64,5... | collective-permute-start | bytes 786440 | tf_op jit(solution)/shard_map/ppermute | solution.py:215

commit v2 on v1

v2 whole, which is shorter than its diff:
```python
import functools

import jax
import jax.numpy as jnp
from jax import lax
from jax.experimental import pallas as pl
from jax.experimental.pallas import tpu as pltpu
from jax.sharding import PartitionSpec as P

D = 1024
HEADS = 8
HEAD_DIM = 64
INNER = 512
HALF = 8
EPSILON = 1e-06
LOG2E = 1.4426950408889634
FAR = 4096.0
BF = jnp.bfloat16
F32 = jnp.float32
MIB = 1 << 20


def normalize(values):
    center = jnp.mean(values, axis=-1, keepdims=True)
    off = values - center
    spread = jnp.mean(off * off, axis=-1, keepdims=True)
    return off * lax.rsqrt(spread + EPSILON)


def store_ranks(ord_ref, block_refs):
    ranks = ord_ref[0].astype(F32).astype(BF)
    natural = lax.broadcasted_iota(jnp.int32, (256, 256), 0)
    m = lax.broadcasted_iota(jnp.int32, (256, 256), 1)
    source = ((m >> 7) * 8 + ((m >> 3) & 7)) * 16 + ((m >> 6) & 1) * 8 + (m & 7)
    quads = jnp.dot(ranks, (natural == source).astype(F32).astype(BF), preferred_element_type=F32)
    rank_row = jnp.concatenate(
        [ranks[0:1].astype(F32), ranks[1:2].astype(F32), ranks[2:3].astype(F32), quads[3:4]], axis=1
    )
    block = jnp.broadcast_to(rank_row, (16, D)).astype(BF)
    for ref, at in block_refs:
        ref[at : at + 16, :] = block


def put_strips(odd, at, left, right, e1, e2):
    e1[at : at + 16, :] = jnp.where(odd, right, left)
    e2[at : at + 16, :] = jnp.where(odd, left, right)


def pack_rows(x_ref, ord_hbm, up, dn, held, ord_ref, sem, strips=()):
    odd = lax.rem(lax.axis_index("cols"), 2) == 1
    copies = [
        pltpu.make_async_copy(x_ref.at[pl.ds(2 * q, 2)], held.at[pl.ds(2 * q, 2)], sem.at[q]) for q in range(8)
    ]
    ranks_copy = pltpu.make_async_copy(ord_hbm, ord_ref, sem.at[8])
    ranks_copy.start()
    for copy in copies:
        copy.start()
    ranks_copy.wait()
    store_ranks(ord_ref, [(dn, 512)] + [(ref, 128) for ref in strips])
    for q, copy in enumerate(copies):
        copy.wait()
        h, t = q // 4, q % 4
        ref = dn if h else up
        rows = [held[2 * q + u].astype(F32) for u in range(2)]
        for j in range(3):
            for u in range(2):
                part = normalize(rows[u][8 + 16 * j : 24 + 16 * j]).astype(BF)
                at = 128 * j + (2 * t + u) * 16
                ref[at : at + 16, :] = part
        left = normalize(jnp.concatenate([rows[0][:8], rows[1][:8]], axis=0)).astype(BF)
        right = normalize(jnp.concatenate([rows[0][56:], rows[1][56:]], axis=0)).astype(BF)
        ref[384 + t * 16 : 400 + t * 16, :] = left
        ref[448 + t * 16 : 464 + t * 16, :] = right
        if strips:
            put_strips(odd, 64 * h + t * 16, left, right, *strips)


def pack_kernel(x_ref, ord_hbm, up, dn, e1, e2, held, ord_ref, sem):
    pack_rows(x_ref, ord_hbm, up, dn, held, ord_ref, sem, (e1, e2))


def is_early():
    return lax.axis_index("cols") < lax.axis_size("cols") // 2


def project_early_kernel(up, dn, e1, e2, w_hbm, p, again, w_ref, sem):
    @pl.when(jnp.logical_not(is_early()))
    def _():
        again[...] = e2[...]

    @pl.when(is_early())
    def _():
        again[...] = e1[...]
        copies = []
        for n in range(3):
            at = pl.ds(INNER * n, INNER)
            copies.append(pltpu.make_async_copy(w_hbm.at[:, at], w_ref.at[:, at], sem.at[n]))
        for copy in copies:
            copy.start()
        for n, copy in enumerate(copies):
            copy.wait()
            at = slice(INNER * n, INNER * n + INNER)
            for h, src in enumerate((up, dn)):
                p[h, :, at] = jnp.dot(src[0:512, :], w_ref[:, at], preferred_element_type=F32).astype(BF)


def project_late_kernel(up, dn, w_ref, p):
    @pl.when(jnp.logical_not(is_early()))
    def _():
        for h, src in enumerate((up, dn)):
            for q in range(2):
                at = slice(256 * q, 256 * q + 256)
                p[h, at, :] = jnp.dot(src[at, :], w_ref[...], preferred_element_type=F32).astype(BF)


def column_of(row, count):
    q = lax.broadcasted_iota(jnp.int32, (count, 128), 0)
    lane = lax.broadcasted_iota(jnp.int32, (count, 128), 1)
    return jnp.sum(jnp.where(q == lane, jnp.broadcast_to(row, (count, 128)), 0.0), axis=1, keepdims=True)


def attend(query, keys, values, allowed):
    count = query.shape[0]
    both = jnp.concatenate([allowed, allowed], axis=0)
    first = lax.broadcasted_iota(jnp.int32, (count, 128), 1) < HEAD_DIM
    ones = jnp.ones((256, 128), BF)
    outs = []
    for g in range(4):
        at = slice(128 * g, 128 * g + 128)
        q = query[:, at]
        zero = jnp.zeros_like(q)
        q = jnp.concatenate([jnp.where(first, q, zero), jnp.where(first, zero, q)], axis=0)
        s = lax.dot_general(q, keys[:, at], (((1,), (1,)), ((), ())), preferred_element_type=F32)
        s = jnp.where(both, s, -jnp.inf)
        top = jnp.max(s, axis=-1, keepdims=True)
        p = jnp.exp2((s - top) * (LOG2E * HEAD_DIM**-0.5)).astype(BF)
        o = jnp.dot(p, jnp.concatenate([values[:, at], ones], axis=1), preferred_element_type=F32)
        number = jnp.where(first, o[:count, :128], o[count:, :128])
        total = jnp.where(first, o[:count, 128:], o[count:, 128:])
        outs.append(number / total)
    return jnp.concatenate(outs, axis=1)


def inner_window(h, j, own, other_kv, rank_row, last, out):
    own_ranks = rank_row[:, 128:] if h == 0 else rank_row[:, :128]
    other_ranks = (rank_row[:, :128] if h == 0 else rank_row[:, 128:]) + jnp.where(last, FAR, 0.0)
    key_ranks = jnp.concatenate([own_ranks, other_ranks], axis=1)
    allowed = key_ranks <= column_of(own_ranks, 128)
    keys = jnp.concatenate([own[:, INNER : 2 * INNER], other_kv[:, :INNER]], axis=0)
    values = jnp.concatenate([own[:, 2 * INNER :], other_kv[:, INNER:]], axis=0)
    out[h, j] = attend(own[:, :INNER], keys, values, allowed).astype(BF)


def last_pair(h):
    size = lax.axis_size("rows")
    return lax.axis_index("rows") == (0 if h == 0 else size - 1)


def by_side(body, p_early, p_late):
    early = is_early()
    pl.when(early)(lambda: body(p_early))
    pl.when(jnp.logical_not(early))(lambda: body(p_late))


def inner_kernel(up, dn, p_early, p_late, w_ref, ord_ref, out, kve):
    by_side(lambda p: inner_windows(up, dn, p, w_ref, ord_ref, out, kve), p_early, p_late)


def inner_windows(up, dn, p, w_ref, ord_ref, out, kve):
    for h, src in enumerate((dn, up)):
        kv = jnp.dot(src[0:512, :], w_ref[:, INNER:], preferred_element_type=F32).astype(BF)
        for j in range(3):
            if h == 0:
                ranks = dn[512:528, 256 * j : 256 * j + 256].astype(F32)[0:1]
            else:
                ranks = ord_ref[0, j : j + 1, :].astype(F32)
            at = slice(128 * j, 128 * j + 128)
            inner_window(h, j, p[h, at, :], kv[at], ranks, last_pair(h), out)
        kve[h, 0] = kv[384:448]
        kve[h, 1] = kv[448:512]


def one_of(cols):
    col = lax.axis_index("cols")
    return functools.reduce(jnp.logical_or, [col == c for c in cols])


def merge_kernel(got_x, got_z, tie, to_up, to_dn):
    del tie
    for e, src in enumerate((got_x, got_z)):
        to_up[64 * e : 64 * e + 64, :] = src[0:64, :]
        to_dn[80 * e : 80 * e + 80, :] = src[64:144, :]


def split_kernel(got_y, tie, to_up, to_dn):
    del tie
    to_up[...] = got_y[0:64, :]
    to_dn[...] = got_y[64:144, :]


def strips_kernel(y_first, y_second, got_x, got_y, got_z, w_ref, tie, kvf):
    del tie
    for e, (src, y_cols) in enumerate(((got_x, y_first), (got_z, y_second))):
        strip = jnp.where(one_of(y_cols), got_y[0:128, :], src[0:128, :])
        kv = jnp.dot(strip, w_ref[:, INNER:], preferred_element_type=F32).astype(BF)
        kvf[e, 0] = kv[0:64]
        kvf[e, 1] = kv[64:128]


def edge_kernel(y_first, y_second, *refs):
    ux, uy, dx, dy, got_x, got_y, got_z, kvf, w_ref, ord_ref = refs[:10]
    dn, p_early, p_late, inner, kve, out, edge = refs[10:]
    ups, downs, besides, corners = [], [], [], []
    for e, (src, y_cols) in enumerate(((got_x, y_first), (got_z, y_second))):
        from_y = one_of(y_cols)
        ups.append(jnp.where(from_y, uy[...], ux[64 * e : 64 * e + 64, :]))
        downs.append(jnp.where(from_y, dy[0:64, :], dx[80 * e : 80 * e + 64, :]))
        corners.append(jnp.where(from_y, dy[64:80, 768:1024], dx[80 * e + 64 : 80 * e + 80, 768:1024]))
        besides.append(jnp.where(from_y, got_y[128:144, 768:1024], src[128:144, 768:1024]))
    col = lax.axis_index("cols")
    odd = lax.rem(col, 2)
    natural = lax.broadcasted_iota(jnp.int32, (256, 256), 0)
    m = lax.broadcasted_iota(jnp.int32, (256, 256), 1)
    source = ((m >> 7) * 8 + ((m >> 3) & 7)) * 16 + ((m >> 6) & 1) * 8 + (m & 7)
    own_ranks = ord_ref[0].astype(F32).astype(BF)
    mine = jnp.dot(own_ranks, (natural == source).astype(F32).astype(BF), preferred_element_type=F32)[3:4]
    diag = jnp.concatenate(downs + ups, axis=0)
    kvd = jnp.dot(diag, w_ref[:, INNER:], preferred_element_type=F32).astype(BF)

    def edges(p):
        above = dn[512:528, 768:1024].astype(F32)[0:1]
        for e, (beside, corner) in enumerate(zip(besides, corners)):
            side = odd if e == 0 else 1 - odd
            is_left = side == 0
            beside = beside.astype(F32)[0:1]
            corner = corner.astype(F32)[0:1]
            last_col = jnp.where(is_left, col == 0, col == lax.axis_size("cols") - 1)
            for h in range(2):
                ranks = jnp.where(is_left, corner, above) if h == 0 else jnp.where(is_left, beside, mine)
                half_own = ranks[:, 128:] if h == 0 else ranks[:, :128]
                half_other = ranks[:, :128] if h == 0 else ranks[:, 128:]
                half_own, half_other = (
                    jnp.where(is_left, jnp.concatenate([x[:, 64:], x[:, :64]], axis=1), x) for x in (half_own, half_other)
                )
                lane = lax.broadcasted_iota(jnp.int32, (1, 128), 1)
                far_col = jnp.where((lane >= 64) & last_col, FAR, 0.0)
                key_ranks = jnp.concatenate(
                    [half_own + far_col, half_other + far_col + jnp.where(last_pair(h), FAR, 0.0)], axis=1
                )
                allowed = key_ranks <= column_of(half_own, 64)
                own = p[h, pl.ds(pl.multiple_of(384 + 64 * side, 64), 64), :]
                near = kve[h, side]
                far = kvf[e, h]
                cross = kvd[128 * h + 64 * e : 128 * h + 64 * e + 64]
                keys = jnp.concatenate(
                    [own[:, INNER : 2 * INNER], far[:, :INNER], near[:, :INNER], cross[:, :INNER]], axis=0
                )
                values = jnp.concatenate([own[:, 2 * INNER :], far[:, INNER:], near[:, INNER:], cross[:, INNER:]], axis=0)
                edge[h, side] = attend(own[:, :INNER], keys, values, allowed)

        for h in range(2):
            for i in range(HALF):
                row = [edge[h, 0, 8 * i : 8 * i + 8]]
                row += [inner[h, j, 16 * i : 16 * i + 16].astype(F32) for j in range(3)]
                row += [edge[h, 1, 8 * i : 8 * i + 8]]
                out[h * HALF + i] = jnp.concatenate(row, axis=0).astype(BF)

    by_side(edges, p_early, p_late)


STRIP_FLOPS = 1000
VMEM = pl.BlockSpec(memory_space=pltpu.VMEM)
ANY = pl.BlockSpec(memory_space=pl.ANY)
HBM = pl.BlockSpec(memory_space=pltpu.HBM)


def call(kernel, outs, args, flops, anywhere=(), scratch=(), aliases=None, limit=24, held=()):
    single = len(outs) == 1
    return pl.pallas_call(
        kernel,
        out_shape=outs[0] if single else tuple(outs),
        in_specs=[HBM if i in held else ANY if i in anywhere else VMEM for i in range(len(args))],
        out_specs=VMEM if single else tuple([VMEM] * len(outs)),
        scratch_shapes=list(scratch),
        input_output_aliases=aliases or {},
        compiler_params=pltpu.CompilerParams(vmem_limit_bytes=limit * MIB),
        cost_estimate=pl.CostEstimate(flops=flops, bytes_accessed=1_000, transcendentals=0),
    )(*args)


def arr(*shape):
    return jax.ShapeDtypeStruct(shape, BF)


def along_rows(value, by):
    size = lax.axis_size("rows")
    return lax.ppermute(value, "rows", [(i, (i + by) % size) for i in range(size)])


def fixed(x):
    return pltpu.with_memory_space_constraint(x, pltpu.HBM)


def per_device(features, qkv_weight, orders):
    cols = lax.axis_size("cols")
    half = cols // 2
    up, dn, e1, e2 = call(
        pack_kernel,
        [arr(512, D), arr(528, D), arr(144, D), arr(144, D)],
        [fixed(features), fixed(orders)],
        1_000,
        held=(0, 1),
        scratch=[pltpu.VMEM((16, 64, D), BF), pltpu.VMEM((1, 4, 256), jnp.int32), pltpu.SemaphoreType.DMA((9,))],
        limit=16,
    )
    first = [(c, (c + 1) % cols if c % 2 else (c - 1) % cols) for c in range(cols)]
    second = [(c, (c - 1) % cols if c % 2 else (c + 1) % cols) for c in range(cols)]
    to_late = [(a, b) for a, b in first if a < half <= b]
    far = [b for _, b in to_late]
    from_far = [(a, b) for a, b in second if a in far]
    y_first, y_second = far, [b for _, b in from_far]
    got_x = lax.ppermute(e1, "cols", [pair for pair in first if pair not in to_late])
    got_up = along_rows(up, -1)
    got_dn = along_rows(dn, 1)
    got_z = lax.ppermute(e2, "cols", [pair for pair in second if pair not in from_far])
    p_early, again = call(
        project_early_kernel,
        [arr(2, 512, 3 * INNER), arr(144, D)],
        [up, dn, e1, e2, fixed(qkv_weight)],
        1_000,
        held=(4,),
        scratch=[pltpu.VMEM((D, 3 * INNER), BF), pltpu.SemaphoreType.DMA((3,))],
    )
    got_y = lax.ppermute(again, "cols", to_late + from_far)
    p_late = call(project_late_kernel, [arr(2, 512, 3 * INNER)], [up, dn, qkv_weight], 1_000)
    inner, kve = call(
        inner_kernel,
        [arr(2, 3, 128, INNER), arr(2, 2, 64, 2 * INNER)],
        [got_up, got_dn, p_early, p_late, qkv_weight, orders],
        1_000,
    )
    to_up, to_dn = call(merge_kernel, [arr(128, D), arr(160, D)], [got_x, got_z, kve], 1_000, anywhere=(2,))
    ux = along_rows(to_up, -1)
    dx = along_rows(to_dn, 1)
    far_up, far_dn = call(split_kernel, [arr(64, D), arr(80, D)], [got_y, to_up], STRIP_FLOPS, anywhere=(1,))
    uy = along_rows(far_up, -1)
    dy = along_rows(far_dn, 1)
    kvf = call(
        functools.partial(strips_kernel, y_first, y_second),
        [arr(2, 2, 64, 2 * INNER)],
        [got_x, got_y, got_z, qkv_weight, far_up],
        1_000,
        anywhere=(4,),
    )
    return call(
        functools.partial(edge_kernel, y_first, y_second),
        [arr(16, 64, INNER)],
        [ux, uy, dx, dy, got_x, got_y, got_z, kvf, qkv_weight, orders, got_dn, p_early, p_late, inner, kve],
        1_000,
        scratch=[pltpu.VMEM((2, 2, 64, INNER), F32)],
    )


def solution(mesh):
    in_specs = (P(("batch", "rows"), "cols", None), P(), P(("batch", "rows"), "cols", None))
    out_specs = P(("batch", "rows"), "cols", None)
    return jax.shard_map(
        per_device, mesh=mesh, in_specs=in_specs, out_specs=out_specs, check_vma=False
    )
```

time: 50 us -> 44.1 us (0.88)
  the two profiles are of different devices: /device:TPU:96 before, /device:TPU:25 now
where the time goes in v2:
time: 44.1 us; the launch traced here: 43.9 us
  starting transfers between devices  17.6 us (40%)
  Pallas kernels  16.4 us (37%)
  waiting for transfers between devices  9.77 us (22%)
    pallas_call x8, Pallas kernels, call(): pl.pallas_call(kernel, out_shape=outs[0] if single else tuple(outs), in_s...  16.4 us
    ppermute x6, starting transfers between devices, along_rows(): lax.ppermute(value, 'rows', [(i, (i + by) % size) for i in range(size)])  7.09 us
    ppermute x6, waiting for transfers between devices, along_rows(): lax.ppermute(value, 'rows', [(i, (i + by) % size) for i in range(size)])  5 us
    ppermute x1, starting transfers between devices, per_device(): lax.ppermute(e2, 'cols', [pair for pair in second if pair not in from_far])  4.95 us
    ppermute x1, waiting for transfers between devices, per_device(): got_y = lax.ppermute(again, 'cols', to_late + from_far)  4.76 us
    ppermute x1, starting transfers between devices, per_device(): got_y = lax.ppermute(again, 'cols', to_late + from_far)  4.25 us
    ppermute x1, starting transfers between devices, per_device(): lax.ppermute(e1, 'cols', [pair for pair in first if pair not in to_late])  1.28 us
  transfers between devices with their start and end apart: 9, of which 3 were waited for; matrix products, arithmetic and copies ran while one was open for 0% of the time, Pallas kernels for 24%

profile of v2, /device:TPU:25, one launch (start us, length us, event | category | flops | bytes accessed | tf_op | source)
XLA Modules:
  0.0 43.9 jit_solution(3591067839359989130)
XLA Ops:
  0.0 2.9 %shard_map.37 = (bf16[512,1024]{1,0:T(8,128)(2,1)S(1)}, bf16[528,1024]{1,0:T(8,128)(2,1)S(1)}, bf16[144,1024]{1,0:T(8,128)(2,1)S(1)}, bf16[144,1024]{1,0:T(8,128)(2,1)S(1)}) custom-call(bf16[16,64,1024]{2,1,0:T(8,128)(2,1)} %x_ref.1, s32[1,4,256]{2,1,0:T(4,128)} %refs_9_.1), custom_call_target="tpu_custom_call" | custom-call | flops 1000 | bytes 1000 | tf_op jit(solution)/shard_map/pallas_call | solution.py:279
  3.0 0.0 copy-start
  3.0 3.1 %collective-permute-start.3 = (bf16[528,1024]{1,0:T(8,128)(2,1)S(1)}, bf16[528,1024]{1,0:T(8,128)(2,1)S(1)}, u32[]{:S(2)}, u32[]{:S(2)}) collective-permute-start(bf16[528,1024]{1,0:T(8,128)(2,1)S(1)} %get-tuple-element.20.dn), channel_id=1, source_target_pairs={{0,8},{8,16},{16,24},{24,32},{32,40},{40,48},{48,56},{56,64},{64,7... | collective-permute-start | bytes 3244040 | tf_op jit(solution)/shard_map/ppermute | solution.py:297
  6.0 0.0 collective-permute-start.2
  6.0 1.3 %collective-permute-start = (bf16[144,1024]{1,0:T(8,128)(2,1)S(1)}, bf16[144,1024]{1,0:T(8,128)(2,1)S(1)}, u32[]{:S(2)}, u32[]{:S(2)}) collective-permute-start(bf16[144,1024]{1,0:T(8,128)(2,1)S(1)} %get-tuple-element.17.e1), channel_id=1, source_target_pairs={{1,2},{2,1},{4,3},{5,6},{6,5},{7,0},{9,10},{10,9},{12,11},{13,14},... | collective-permute-start | bytes 884744 | tf_op jit(solution)/shard_map/ppermute | solution.py:322
  7.3 4.9 %collective-permute-start.1 = (bf16[144,1024]{1,0:T(8,128)(2,1)S(1)}, bf16[144,1024]{1,0:T(8,128)(2,1)S(1)}, u32[]{:S(2)}, u32[]{:S(2)}) collective-permute-start(bf16[144,1024]{1,0:T(8,128)(2,1)S(1)} %get-tuple-element.18.e2), channel_id=1, source_target_pairs={{0,1},{1,0},{2,3},{3,2},{5,4},{6,7},{8,9},{9,8},{10,11},{11,10},{1... | collective-permute-start | bytes 884744 | tf_op jit(solution)/shard_map/ppermute | solution.py:325
  12.3 5.0 %shard_map.38 = (bf16[2,512,1536]{2,1,0:T(8,128)(2,1)S(1)}, bf16[144,1024]{1,0:T(8,128)(2,1)S(1)}) custom-call(bf16[512,1024]{1,0:T(8,128)(2,1)S(1)} %get-tuple-element.19.up, bf16[528,1024]{1,0:T(8,128)(2,1)S(1)} %get-tuple-element.20.dn, bf16[144,1024]{1,0:T(8,128)(2,1)S(1)} %get-tuple-element.17.e1, bf16[144,1024]{1,0:T(8,128)(2,1)S(1)} %get-tuple-element.18.e2, ...), custom_call_target="tpu_custom_call" | custom-call | flops 1000 | bytes 1000 | tf_op jit(solution)/shard_map/pallas_call | solution.py:279
  17.3 0.0 copy-start.1
  17.3 4.2 %collective-permute-start.5 = (bf16[144,1024]{1,0:T(8,128)(2,1)S(1)}, bf16[144,1024]{1,0:T(8,128)(2,1)S(1)}, u32[]{:S(2)}, u32[]{:S(2)}) collective-permute-start(bf16[144,1024]{1,0:T(8,128)(2,1)S(1)} %get-tuple-element.24), channel_id=1, source_target_pairs={{0,7},{3,4},{4,5},{7,6},{8,15},{11,12},{12,13},{15,14},{16,23},{19... | collective-permute-start | bytes 884744 | tf_op jit(solution)/shard_map/ppermute | solution.py:334
  21.6 0.2 collective-permute-done.2.up
  21.8 0.0 collective-permute-done.3.dn.refs_10_
  21.8 4.7 %shard_map.40 = (bf16[2,3,128,512]{3,2,1,0:T(8,128)(2,1)S(1)}, bf16[2,2,64,1024]{3,2,1,0:T(8,128)(2,1)S(1)}) custom-call(bf16[512,1024]{1,0:T(8,128)(2,1)S(1)} %collective-permute-done.2.up, bf16[528,1024]{1,0:T(8,128)(2,1)S(1)} %collective-permute-done.3.dn.refs_10_, bf16[2,512,1536]{2,1,0:T(8,128)(2,1)S(1)} %get-tuple-element.21.p_early.refs_11_, ...), custom_call_target="tpu_custom_call" | custom-call | flops 1000 | bytes 1000 | tf_op jit(solution)/shard_map/pallas_call | solution.py:279
  26.5 0.0 collective-permute-done.got_x.refs_4_
  26.5 0.0 collective-permute-done.1.got_z.refs_6_
  26.5 3.1 %collective-permute-start.7 = (bf16[160,1024]{1,0:T(8,128)(2,1)S(1)}, bf16[160,1024]{1,0:T(8,128)(2,1)S(1)}, u32[]{:S(2)}, u32[]{:S(2)}) collective-permute-start(bf16[160,1024]{1,0:T(8,128)(2,1)S(1)} %get-tuple-element.26), channel_id=1, source_target_pairs={{0,8},{8,16},{16,24},{24,32},{32,40},{40,48},{48,56},{56,64},{64,7... | collective-permute-start | bytes 983048 | tf_op jit(solution)/shard_map/ppermute | solution.py:297
  29.6 0.0 collective-permute-start.4
  29.6 4.8 %collective-permute-done.5.got_y.refs_5_ = bf16[144,1024]{1,0:T(8,128)(2,1)S(1)} collective-permute-done((bf16[144,1024]{1,0:T(8,128)(2,1)S(1)}, bf16[144,1024]{1,0:T(8,128)(2,1)S(1)}, u32[]{:S(2)}, u32[]{:S(2)}) %collective-permute-start.5) | collective-permute-done | bytes 294944 | tf_op jit(solution)/shard_map/ppermute | solution.py:334
  34.4 0.9 %collective-permute-start.8 = (bf16[80,1024]{1,0:T(8,128)(2,1)S(1)}, bf16[80,1024]{1,0:T(8,128)(2,1)S(1)}, u32[]{:S(2)}, u32[]{:S(2)}) collective-permute-start(bf16[80,1024]{1,0:T(8,128)(2,1)S(1)} %get-tuple-element.27), channel_id=1, source_target_pairs={{0,8},{8,16},{16,24},{24,32},{32,40},{40,48},{48,56},{56,64},{64,7... | collective-permute-start | bytes 491528 | tf_op jit(solution)/shard_map/ppermute | solution.py:297
  35.3 0.8 %shard_map.43.refs_7_ = bf16[2,2,64,1024]{3,2,1,0:T(8,128)(2,1)S(1)} custom-call(bf16[144,1024]{1,0:T(8,128)(2,1)S(1)} %collective-permute-done.got_x.refs_4_, bf16[144,1024]{1,0:T(8,128)(2,1)S(1)} %collective-permute-done.5.got_y.refs_5_, bf16[144,1024]{1,0:T(8,128)(2,1)S(1)} %collective-permute-done.1.got_z.refs_6_, bf16[1024,1536]{1,0:T(8,128)(2,1)S(1)} %copy-done, ...), custom_call_target="tpu_custom_call" | custom-call | flops 1000 | bytes 1000 | tf_op jit(solution)/shard_map/pallas_call | solution.py:279
  36.1 4.8 %collective-permute-done.6.refs_1_ = bf16[64,1024]{1,0:T(8,128)(2,1)S(1)} collective-permute-done((bf16[64,1024]{1,0:T(8,128)(2,1)S(1)}, bf16[64,1024]{1,0:T(8,128)(2,1)S(1)}, u32[]{:S(2)}, u32[]{:S(2)}) %collective-permute-start.6) | collective-permute-done | bytes 131104 | tf_op jit(solution)/shard_map/ppermute | solution.py:297
  40.9 0.0 collective-permute-done.8.refs_3_
  40.9 0.0 collective-permute-done.4.refs_0_
  40.9 0.0 collective-permute-done.7.refs_2_
  40.9 2.9 %shard_map.44 = bf16[16,64,512]{2,1,0:T(8,128)(2,1)} custom-call(bf16[128,1024]{1,0:T(8,128)(2,1)S(1)} %collective-permute-done.4.refs_0_, bf16[64,1024]{1,0:T(8,128)(2,1)S(1)} %collective-permute-done.6.refs_1_, bf16[160,1024]{1,0:T(8,128)(2,1)S(1)} %collective-permute-done.7.refs_2_, bf16[80,1024]{1,0:T(8,128)(2,1)S(1)} %collective-permute-done.8.refs_3_, ...), custom_call_target="tpu_custom_call" | custom-call | flops 1000 | bytes 1000 | tf_op jit(solution)/shard_map/pallas_call | solution.py:279
  (6 shorter events, 0.1 us)
Async XLA Ops:
  3.0 18.6 %copy-start = (bf16[1024,1536]{1,0:T(8,128)(2,1)S(1)}, bf16[1024,1536]{1,0:T(8,128)(2,1)}, u32[]{:S(2)}) copy-start(bf16[1024,1536]{1,0:T(8,128)(2,1)} %refs_8_.1) | copy-start | bytes 9437188
  3.0 18.8 %collective-permute-start.3 = (bf16[528,1024]{1,0:T(8,128)(2,1)S(1)}, bf16[528,1024]{1,0:T(8,128)(2,1)S(1)}, u32[]{:S(2)}, u32[]{:S(2)}) collective-permute-start(bf16[528,1024]{1,0:T(8,128)(2,1)S(1)} %get-tuple-element.20.dn), channel_id=1, source_target_pairs={{0,8},{8,16},{16,24},{24,32},{32,40},{40,48},{48,56},{56,64},{64,7... | collective-permute-start | bytes 3244040 | tf_op jit(solution)/shard_map/ppermute | solution.py:297
  6.0 15.7 %collective-permute-start.2 = (bf16[512,1024]{1,0:T(8,128)(2,1)S(1)}, bf16[512,1024]{1,0:T(8,128)(2,1)S(1)}, u32[]{:S(2)}, u32[]{:S(2)}) collective-permute-start(bf16[512,1024]{1,0:T(8,128)(2,1)S(1)} %get-tuple-element.19.up), channel_id=1, source_target_pairs={{0,120},{8,0},{16,8},{24,16},{32,24},{40,32},{48,40},{56,48},{64,5... | collective-permute-start | bytes 3145736 | tf_op jit(solution)/shard_map/ppermute | solution.py:297
  6.0 20.4 %collective-permute-start = (bf16[144,1024]{1,0:T(8,128)(2,1)S(1)}, bf16[144,1024]{1,0:T(8,128)(2,1)S(1)}, u32[]{:S(2)}, u32[]{:S(2)}) collective-permute-start(bf16[144,1024]{1,0:T(8,128)(2,1)S(1)} %get-tuple-element.17.e1), channel_id=1, source_target_pairs={{1,2},{2,1},{4,3},{5,6},{6,5},{7,0},{9,10},{10,9},{12,11},{13,14},... | collective-permute-start | bytes 884744 | tf_op jit(solution)/shard_map/ppermute | solution.py:322
  7.3 19.1 %collective-permute-start.1 = (bf16[144,1024]{1,0:T(8,128)(2,1)S(1)}, bf16[144,1024]{1,0:T(8,128)(2,1)S(1)}, u32[]{:S(2)}, u32[]{:S(2)}) collective-permute-start(bf16[144,1024]{1,0:T(8,128)(2,1)S(1)} %get-tuple-element.18.e2), channel_id=1, source_target_pairs={{0,1},{1,0},{2,3},{3,2},{5,4},{6,7},{8,9},{9,8},{10,11},{11,10},{1... | collective-permute-start | bytes 884744 | tf_op jit(solution)/shard_map/ppermute | solution.py:325
  17.3 4.5 %copy-start.1 = (s32[1,4,256]{2,1,0:T(4,128)S(1)}, s32[1,4,256]{2,1,0:T(4,128)}, u32[]{:S(2)}) copy-start(s32[1,4,256]{2,1,0:T(4,128)} %refs_9_.1) | copy-start | bytes 12292
  17.3 17.1 %collective-permute-start.5 = (bf16[144,1024]{1,0:T(8,128)(2,1)S(1)}, bf16[144,1024]{1,0:T(8,128)(2,1)S(1)}, u32[]{:S(2)}, u32[]{:S(2)}) collective-permute-start(bf16[144,1024]{1,0:T(8,128)(2,1)S(1)} %get-tuple-element.24), channel_id=1, source_target_pairs={{0,7},{3,4},{4,5},{7,6},{8,15},{11,12},{12,13},{15,14},{16,23},{19... | collective-permute-start | bytes 884744 | tf_op jit(solution)/shard_map/ppermute | solution.py:334
  26.5 14.4 %collective-permute-start.7 = (bf16[160,1024]{1,0:T(8,128)(2,1)S(1)}, bf16[160,1024]{1,0:T(8,128)(2,1)S(1)}, u32[]{:S(2)}, u32[]{:S(2)}) collective-permute-start(bf16[160,1024]{1,0:T(8,128)(2,1)S(1)} %get-tuple-element.26), channel_id=1, source_target_pairs={{0,8},{8,16},{16,24},{24,32},{32,40},{40,48},{48,56},{56,64},{64,7... | collective-permute-start | bytes 983048 | tf_op jit(solution)/shard_map/ppermute | solution.py:297
  29.6 11.3 %collective-permute-start.4 = (bf16[128,1024]{1,0:T(8,128)(2,1)S(1)}, bf16[128,1024]{1,0:T(8,128)(2,1)S(1)}, u32[]{:S(2)}, u32[]{:S(2)}) collective-permute-start(bf16[128,1024]{1,0:T(8,128)(2,1)S(1)} %get-tuple-element.23.tie), channel_id=1, source_target_pairs={{0,120},{8,0},{16,8},{24,16},{32,24},{40,32},{48,40},{56,48},{64,5... | collective-permute-start | bytes 786440 | tf_op jit(solution)/shard_map/ppermute | solution.py:297
  34.4 6.5 %collective-permute-start.8 = (bf16[80,1024]{1,0:T(8,128)(2,1)S(1)}, bf16[80,1024]{1,0:T(8,128)(2,1)S(1)}, u32[]{:S(2)}, u32[]{:S(2)}) collective-permute-start(bf16[80,1024]{1,0:T(8,128)(2,1)S(1)} %get-tuple-element.27), channel_id=1, source_target_pairs={{0,8},{8,16},{16,24},{24,32},{32,40},{40,48},{48,56},{56,64},{64,7... | collective-permute-start | bytes 491528 | tf_op jit(solution)/shard_map/ppermute | solution.py:297
  35.3 5.6 %collective-permute-start.6 = (bf16[64,1024]{1,0:T(8,128)(2,1)S(1)}, bf16[64,1024]{1,0:T(8,128)(2,1)S(1)}, u32[]{:S(2)}, u32[]{:S(2)}) collective-permute-start(bf16[64,1024]{1,0:T(8,128)(2,1)S(1)} %get-tuple-element.25.tie), channel_id=1, source_target_pairs={{0,120},{8,0},{16,8},{24,16},{32,24},{40,32},{48,40},{56,48},{64,5... | collective-permute-start | bytes 393224 | tf_op jit(solution)/shard_map/ppermute | solution.py:297

commit v3 on v2

v3 whole, which is shorter than its diff:
```python
import functools

import jax
import jax.numpy as jnp
from jax import lax
from jax.experimental import pallas as pl
from jax.experimental.pallas import tpu as pltpu
from jax.sharding import PartitionSpec as P

D = 1024
HEADS = 8
HEAD_DIM = 64
INNER = 512
HALF = 8
EPSILON = 1e-06
LOG2E = 1.4426950408889634
FAR = 4096.0
BF = jnp.bfloat16
F32 = jnp.float32
MIB = 1 << 20


def normalize(values):
    center = jnp.mean(values, axis=-1, keepdims=True)
    off = values - center
    spread = jnp.mean(off * off, axis=-1, keepdims=True)
    return off * lax.rsqrt(spread + EPSILON)


def put_tokens(ref, per, at, values):
    for k in range(8):
        ref[per * k + at : per * k + at + values.shape[0], :] = values[:, 128 * k : 128 * k + 128]


def get_tokens(ref, per, at, count):
    return jnp.concatenate([ref[per * k + at : per * k + at + count, :] for k in range(8)], axis=1)


def get_ranks(block):
    block = block.astype(F32)
    return jnp.concatenate([block[0:1], block[8:9]], axis=1)


def store_ranks(ord_ref, dn, strips):
    ranks = ord_ref[0].astype(F32).astype(BF)
    natural = lax.broadcasted_iota(jnp.int32, (256, 256), 0)
    m = lax.broadcasted_iota(jnp.int32, (256, 256), 1)
    source = ((m >> 7) * 8 + ((m >> 3) & 7)) * 16 + ((m >> 6) & 1) * 8 + (m & 7)
    quads = jnp.dot(ranks, (natural == source).astype(F32).astype(BF), preferred_element_type=F32)
    rank_row = jnp.concatenate(
        [ranks[0:1].astype(F32), ranks[1:2].astype(F32), ranks[2:3].astype(F32), quads[3:4]], axis=1
    )
    dn[512:528, :] = jnp.broadcast_to(rank_row, (16, D)).astype(BF)
    halves = [jnp.broadcast_to(quads[3:4, 128 * n : 128 * n + 128], (8, 128)) for n in range(2)]
    for ref in strips:
        ref[1024:1040, :] = jnp.concatenate(halves, axis=0).astype(BF)


def put_strips(odd, at, left, right, e1, e2):
    put_tokens(e1, 128, at, jnp.where(odd, right, left))
    put_tokens(e2, 128, at, jnp.where(odd, left, right))


def pack_rows(x_ref, ord_hbm, up, dn, held, ord_ref, sem, strips=()):
    odd = lax.rem(lax.axis_index("cols"), 2) == 1
    copies = [
        pltpu.make_async_copy(x_ref.at[pl.ds(4 * q, 4)], held.at[pl.ds(4 * q, 4)], sem.at[q]) for q in range(4)
    ]
    ranks_copy = pltpu.make_async_copy(ord_hbm, ord_ref, sem.at[4])
    ranks_copy.start()
    for copy in copies:
        copy.start()
    ranks_copy.wait()
    store_ranks(ord_ref, dn, strips)
    for q in range(8):
        if q % 2 == 0:
            copies[q // 2].wait()
        h, t = q // 4, q % 4
        ref = dn if h else up
        lefts, rights = [], []
        for u in range(2):
            before = None
            for k in range(4):
                part = normalize(held[2 * q + u, 16 * k : 16 * k + 16, :].astype(F32))
                if k == 0:
                    lefts.append(part[:8])
                else:
                    at = 128 * (k - 1) + (2 * t + u) * 16
                    ref[at : at + 16, :] = jnp.concatenate([before, part[:8]], axis=0).astype(BF)
                before = part[8:]
            rights.append(before)
        left = jnp.concatenate(lefts, axis=0).astype(BF)
        right = jnp.concatenate(rights, axis=0).astype(BF)
        ref[384 + t * 16 : 400 + t * 16, :] = left
        ref[448 + t * 16 : 464 + t * 16, :] = right
        put_strips(odd, 64 * h + t * 16, left, right, *strips)


def pack_kernel(x_ref, ord_hbm, up, dn, e1, e2, held, ord_ref, sem):
    pack_rows(x_ref, ord_hbm, up, dn, held, ord_ref, sem, (e1, e2))


def is_early():
    return lax.axis_index("cols") < lax.axis_size("cols") // 2


def project_early_kernel(up, dn, e1, w_hbm, p, e1_again, w_ref, sem):
    @pl.when(is_early())
    def _():
        e1_again[...] = e1[...]
        copies = []
        for n in range(3):
            at = pl.ds(INNER * n, INNER)
            copies.append(pltpu.make_async_copy(w_hbm.at[:, at], w_ref.at[:, at], sem.at[n]))
        for copy in copies:
            copy.start()
        for n, copy in enumerate(copies):
            copy.wait()
            at = slice(INNER * n, INNER * n + INNER)
            for h, src in enumerate((up, dn)):
                p[h, :, at] = jnp.dot(src[0:512, :], w_ref[:, at], preferred_element_type=F32).astype(BF)


def hold_kernel(value, tie, same):
    del tie
    same[...] = value[...]


def project_late_kernel(up, dn, w_ref, tie, p):
    del tie

    @pl.when(jnp.logical_not(is_early()))
    def _():
        for h, src in enumerate((up, dn)):
            for q in range(2):
                at = slice(256 * q, 256 * q + 256)
                p[h, at, :] = jnp.dot(src[at, :], w_ref[...], preferred_element_type=F32).astype(BF)


def column_of(row, count):
    q = lax.broadcasted_iota(jnp.int32, (count, 128), 0)
    lane = lax.broadcasted_iota(jnp.int32, (count, 128), 1)
    return jnp.sum(jnp.where(q == lane, jnp.broadcast_to(row, (count, 128)), 0.0), axis=1, keepdims=True)


def attend(query, keys, values, allowed):
    count = query.shape[0]
    both = jnp.concatenate([allowed, allowed], axis=0)
    first = lax.broadcasted_iota(jnp.int32, (count, 128), 1) < HEAD_DIM
    ones = jnp.ones((256, 128), BF)
    outs = []
    for g in range(4):
        at = slice(128 * g, 128 * g + 128)
        q = query[:, at]
        zero = jnp.zeros_like(q)
        q = jnp.concatenate([jnp.where(first, q, zero), jnp.where(first, zero, q)], axis=0)
        s = lax.dot_general(q, keys[:, at], (((1,), (1,)), ((), ())), preferred_element_type=F32)
        s = jnp.where(both, s, -jnp.inf)
        top = jnp.max(s, axis=-1, keepdims=True)
        p = jnp.exp2((s - top) * (LOG2E * HEAD_DIM**-0.5)).astype(BF)
        o = jnp.dot(p, jnp.concatenate([values[:, at], ones], axis=1), preferred_element_type=F32)
        number = jnp.where(first, o[:count, :128], o[count:, :128])
        total = jnp.where(first, o[:count, 128:], o[count:, 128:])
        outs.append(number / total)
    return jnp.concatenate(outs, axis=1)


def inner_window(h, j, own, other_kv, rank_row, last, out):
    own_ranks = rank_row[:, 128:] if h == 0 else rank_row[:, :128]
    other_ranks = (rank_row[:, :128] if h == 0 else rank_row[:, 128:]) + jnp.where(last, FAR, 0.0)
    key_ranks = jnp.concatenate([own_ranks, other_ranks], axis=1)
    allowed = key_ranks <= column_of(own_ranks, 128)
    keys = jnp.concatenate([own[:, INNER : 2 * INNER], other_kv[:, :INNER]], axis=0)
    values = jnp.concatenate([own[:, 2 * INNER :], other_kv[:, INNER:]], axis=0)
    out[h, j] = attend(own[:, :INNER], keys, values, allowed).astype(BF)


def last_pair(h):
    size = lax.axis_size("rows")
    return lax.axis_index("rows") == (0 if h == 0 else size - 1)


def by_side(body, p_early, p_late):
    early = is_early()
    pl.when(early)(lambda: body(p_early))
    pl.when(jnp.logical_not(early))(lambda: body(p_late))


def inner_kernel(up, dn, p_early, p_late, w_ref, ord_ref, out, kve):
    by_side(lambda p: inner_windows(up, dn, p, w_ref, ord_ref, out, kve), p_early, p_late)


def inner_windows(up, dn, p, w_ref, ord_ref, out, kve):
    for h, src in enumerate((dn, up)):
        kv = jnp.dot(src[0:512, :], w_ref[:, INNER:], preferred_element_type=F32).astype(BF)
        for j in range(3):
            if h == 0:
                ranks = dn[512:528, 256 * j : 256 * j + 256].astype(F32)[0:1]
            else:
                ranks = ord_ref[0, j : j + 1, :].astype(F32)
            at = slice(128 * j, 128 * j + 128)
            inner_window(h, j, p[h, at, :], kv[at], ranks, last_pair(h), out)
        kve[h, 0] = kv[384:448]
        kve[h, 1] = kv[448:512]


def one_of(cols):
    col = lax.axis_index("cols")
    return functools.reduce(jnp.logical_or, [col == c for c in cols])


def choose_kernel(far, got_x, got_y, e1):
    e1[...] = jnp.where(one_of(far), got_y[...], got_x[...])


def merge_kernel(first, second, to_up, to_dn):
    for e, src in enumerate((first, second)):
        put_tokens(to_up, 128, 64 * e, get_tokens(src, 128, 0, 64))
        put_tokens(to_dn, 128, 64 * e, get_tokens(src, 128, 64, 64))
        to_dn[1024 + 16 * e : 1040 + 16 * e, :] = src[1024:1040, :]


def strips_kernel(first, second, w_ref, tie, kvf):
    del tie
    for e, src in enumerate((first, second)):
        kv = jnp.dot(get_tokens(src, 128, 0, 128), w_ref[:, INNER:], preferred_element_type=F32).astype(BF)
        kvf[e, 0] = kv[0:64]
        kvf[e, 1] = kv[64:128]


def edge_kernel(up, down, first, second, kvf, w_ref, own_strip, dn, p_early, p_late, inner, kve, out_hbm, edge, out, sem):
    ups = [get_tokens(up, 128, 64 * e, 64) for e in range(2)]
    downs = [get_tokens(down, 128, 64 * e, 64) for e in range(2)]
    corners = [get_ranks(down[1024 + 16 * e : 1040 + 16 * e, :]) for e in range(2)]
    besides = [get_ranks(src[1024:1040, :]) for src in (first, second)]
    diags = jnp.concatenate(downs + ups, axis=0)
    kvd = jnp.dot(diags, w_ref[:, INNER:], preferred_element_type=F32).astype(BF)
    mine = get_ranks(own_strip[1024:1040, :])
    copies = [pltpu.make_async_copy(out.at[pl.ds(8 * h, 8)], out_hbm.at[pl.ds(8 * h, 8)], sem.at[h]) for h in range(2)]
    col = lax.axis_index("cols")
    odd = lax.rem(col, 2)

    def edges(p):
        above = dn[512:528, 768:1024].astype(F32)[0:1]
        lane = lax.broadcasted_iota(jnp.int32, (1, 128), 1)
        for h in range(2):
            for e, (beside, corner) in enumerate(zip(besides, corners)):
                side = odd if e == 0 else 1 - odd
                is_left = side == 0
                last_col = jnp.where(is_left, col == 0, col == lax.axis_size("cols") - 1)
                ranks = jnp.where(is_left, corner, above) if h == 0 else jnp.where(is_left, beside, mine)
                half_own = ranks[:, 128:] if h == 0 else ranks[:, :128]
                half_other = ranks[:, :128] if h == 0 else ranks[:, 128:]
                half_own, half_other = (
                    jnp.where(is_left, jnp.concatenate([x[:, 64:], x[:, :64]], axis=1), x) for x in (half_own, half_other)
                )
                far_col = jnp.where((lane >= 64) & last_col, FAR, 0.0)
                key_ranks = jnp.concatenate(
                    [half_own + far_col, half_other + far_col + jnp.where(last_pair(h), FAR, 0.0)], axis=1
                )
                allowed = key_ranks <= column_of(half_own, 64)
                own = p[h, pl.ds(pl.multiple_of(384 + 64 * side, 64), 64), :]
                near = kve[h, side]
                far = kvf[e, h]
                cross = kvd[128 * h + 64 * e : 128 * h + 64 * e + 64]
                keys = jnp.concatenate(
                    [own[:, INNER : 2 * INNER], far[:, :INNER], near[:, :INNER], cross[:, :INNER]], axis=0
                )
                values = jnp.concatenate([own[:, 2 * INNER :], far[:, INNER:], near[:, INNER:], cross[:, INNER:]], axis=0)
                edge[side] = attend(own[:, :INNER], keys, values, allowed)
            for i in range(HALF):
                row = [edge[0, 8 * i : 8 * i + 8]]
                row += [inner[h, j, 16 * i : 16 * i + 16].astype(F32) for j in range(3)]
                row += [edge[1, 8 * i : 8 * i + 8]]
                out[h * HALF + i] = jnp.concatenate(row, axis=0).astype(BF)
            copies[h].start()
        for copy in copies:
            copy.wait()

    by_side(edges, p_early, p_late)


STRIP_FLOPS = 1000
MERGE_FLOPS = 1_000_000_000
VMEM = pl.BlockSpec(memory_space=pltpu.VMEM)
ANY = pl.BlockSpec(memory_space=pl.ANY)
HBM = pl.BlockSpec(memory_space=pltpu.HBM)


def call(kernel, outs, args, flops, anywhere=(), scratch=(), aliases=None, limit=24, held=(), to_hbm=False):
    single = len(outs) == 1
    return pl.pallas_call(
        kernel,
        out_shape=outs[0] if single else tuple(outs),
        in_specs=[HBM if i in held else ANY if i in anywhere else VMEM for i in range(len(args))],
        out_specs=HBM if to_hbm else VMEM if single else tuple([VMEM] * len(outs)),
        scratch_shapes=list(scratch),
        input_output_aliases=aliases or {},
        compiler_params=pltpu.CompilerParams(vmem_limit_bytes=limit * MIB),
        cost_estimate=pl.CostEstimate(flops=flops, bytes_accessed=1_000, transcendentals=0),
    )(*args)


def arr(*shape):
    return jax.ShapeDtypeStruct(shape, BF)


def along_rows(value, by):
    size = lax.axis_size("rows")
    return lax.ppermute(value, "rows", [(i, (i + by) % size) for i in range(size)])


def fixed(x):
    return pltpu.with_memory_space_constraint(x, pltpu.HBM)


def per_device(features, qkv_weight, orders):
    cols = lax.axis_size("cols")
    half = cols // 2
    up, dn, e1, e2 = call(
        pack_kernel,
        [arr(512, D), arr(528, D), arr(1040, 128), arr(1040, 128)],
        [fixed(features), fixed(orders)],
        1_000,
        held=(0, 1),
        scratch=[pltpu.VMEM((16, 64, D), BF), pltpu.VMEM((1, 4, 256), jnp.int32), pltpu.SemaphoreType.DMA((5,))],
        limit=16,
    )
    first = [(c, (c + 1) % cols if c % 2 else (c - 1) % cols) for c in range(cols)]
    second = [(c, (c - 1) % cols if c % 2 else (c + 1) % cols) for c in range(cols)]
    to_late = [(a, b) for a, b in first if a < half <= b]
    far = [b for _, b in to_late]
    got_x = lax.ppermute(e1, "cols", [pair for pair in first if pair not in to_late])
    got_up = along_rows(up, -1)
    got_dn = along_rows(dn, 1)
    p_early, again = call(
        project_early_kernel,
        [arr(2, 512, 3 * INNER), arr(1040, 128)],
        [up, dn, e1, fixed(qkv_weight)],
        1_000,
        held=(3,),
        scratch=[pltpu.VMEM((D, 3 * INNER), BF), pltpu.SemaphoreType.DMA((3,))],
    )
    got_y = lax.ppermute(again, "cols", to_late)
    p_late = call(
        project_late_kernel, [arr(2, 512, 3 * INNER)], [up, dn, qkv_weight, again], 1_000, anywhere=(3,)
    )
    e2_again = call(hold_kernel, [arr(1040, 128)], [e2, p_late], 1_000, anywhere=(1,))
    got_z = lax.ppermute(e2_again, "cols", second)
    inner, kve = call(
        inner_kernel,
        [arr(2, 3, 128, INNER), arr(2, 2, 64, 2 * INNER)],
        [got_up, got_dn, p_early, p_late, qkv_weight, orders],
        1_000,
    )
    got_x = call(hold_kernel, [arr(1040, 128)], [got_x, kve], MERGE_FLOPS, anywhere=(1,))
    got_e1 = call(functools.partial(choose_kernel, far), [arr(1040, 128)], [got_x, got_y], MERGE_FLOPS)
    to_up, to_dn = call(merge_kernel, [arr(1024, 128), arr(1056, 128)], [got_e1, got_z], 1_000)
    hop_up = along_rows(to_up, -1)
    hop_dn = along_rows(to_dn, 1)
    kvf = call(
        strips_kernel, [arr(2, 2, 64, 2 * INNER)], [got_e1, got_z, qkv_weight, to_up], STRIP_FLOPS, anywhere=(3,)
    )
    return call(
        edge_kernel,
        [arr(16, 64, INNER)],
        [hop_up, hop_dn, got_e1, got_z, kvf, qkv_weight, e1, got_dn, p_early, p_late, inner, kve],
        1_000,
        scratch=[pltpu.VMEM((2, 64, INNER), F32), pltpu.VMEM((16, 64, INNER), BF), pltpu.SemaphoreType.DMA((2,))],
        to_hbm=True,
    )


def solution(mesh):
    in_specs = (P(("batch", "rows"), "cols", None), P(), P(("batch", "rows"), "cols", None))
    out_specs = P(("batch", "rows"), "cols", None)
    return jax.shard_map(
        per_device, mesh=mesh, in_specs=in_specs, out_specs=out_specs, check_vma=False
    )
```

time: 44.1 us -> 42.5 us (0.964)
  starting transfers between devices: 17.6 us -> 15 us
  waiting for transfers between devices: 9.77 us -> 11.1 us
  Pallas kernels: 16.4 us -> 15.8 us
    ppermute x6 -> x4, starting transfers between devices: 7.09 us -> 3.96 us  [along_rows(): lax.ppermute(value, 'rows', [(i, (i + by) % size) for i in range(size)])]
    ppermute x6 -> x4, waiting for transfers between devices: 5 us -> 6.29 us  [along_rows(): lax.ppermute(value, 'rows', [(i, (i + by) % size) for i in range(size)])]
    pallas_call x8 -> x10, Pallas kernels: 16.4 us -> 15.8 us  [call(): pl.pallas_call(kernel, out_shape=outs[0] if single else tuple(outs), in_s...]
    ppermute x2, starting transfers between devices: 9.19 us -> 9.8 us  [the longest x1 7.88 us: per_device(): got_y = lax.ppermute(again, 'cols', to_late)]
  transfers between devices with their start and end apart: 9 -> 7, of which waited for: 3 -> 2; matrix products, arithmetic and copies ran while one was open for 0% -> 0% of each run, Pallas kernels for 24% -> 25%
where the time goes in v3:
time: 42.5 us; the launch traced here: 42.3 us
  Pallas kernels  15.8 us (37%)
  starting transfers between devices  15 us (35%)
  waiting for transfers between devices  11.1 us (26%)
    pallas_call x10, Pallas kernels, call(): pl.pallas_call(kernel, out_shape=outs[0] if single else tuple(outs), in_s...  15.8 us
    ppermute x1, starting transfers between devices, per_device(): got_y = lax.ppermute(again, 'cols', to_late)  7.88 us
    ppermute x4, waiting for transfers between devices, along_rows(): lax.ppermute(value, 'rows', [(i, (i + by) % size) for i in range(size)])  6.29 us
    ppermute x1, waiting for transfers between devices, per_device(): got_y = lax.ppermute(again, 'cols', to_late)  4.85 us
    ppermute x4, starting transfers between devices, along_rows(): lax.ppermute(value, 'rows', [(i, (i + by) % size) for i in range(size)])  3.96 us
    ppermute x1, starting transfers between devices, per_device(): got_z = lax.ppermute(e2_again, 'cols', second)  1.92 us
    ppermute x1, starting transfers between devices, per_device(): lax.ppermute(e1, 'cols', [pair for pair in first if pair not in to_late])  1.28 us
  transfers between devices with their start and end apart: 7, of which 2 were waited for; matrix products, arithmetic and copies ran while one was open for 0% of the time, Pallas kernels for 25%

profile of v3, /device:TPU:25, one launch (start us, length us, event | category | flops | bytes accessed | tf_op | source)
XLA Modules:
  0.0 42.3 jit_solution(13149653045935362102)
XLA Ops:
  0.0 2.4 %shard_map.37 = (bf16[512,1024]{1,0:T(8,128)(2,1)S(1)}, bf16[528,1024]{1,0:T(8,128)(2,1)S(1)}, bf16[1040,128]{1,0:T(8,128)(2,1)S(1)}, bf16[1040,128]{1,0:T(8,128)(2,1)S(1)}) custom-call(bf16[16,64,1024]{2,1,0:T(8,128)(2,1)} %x_ref.1, s32[1,4,256]{2,1,0:T(4,128)} %ord_ref.1), custom_call_target="tpu_custom_call" | custom-call | flops 1000 | bytes 1000 | tf_op jit(solution)/shard_map/pallas_call | solution.py:292
  2.4 0.0 copy-start
  2.4 3.1 %collective-permute-start.2 = (bf16[528,1024]{1,0:T(8,128)(2,1)S(1)}, bf16[528,1024]{1,0:T(8,128)(2,1)S(1)}, u32[]{:S(2)}, u32[]{:S(2)}) collective-permute-start(bf16[528,1024]{1,0:T(8,128)(2,1)S(1)} %get-tuple-element.17.dn), channel_id=1, source_target_pairs={{0,8},{8,16},{16,24},{24,32},{32,40},{40,48},{48,56},{56,64},{64,7... | collective-permute-start | bytes 3244040 | tf_op jit(solution)/shard_map/ppermute | solution.py:310
  5.5 0.0 collective-permute-start.1
  5.5 1.3 %collective-permute-start = (bf16[1040,128]{1,0:T(8,128)(2,1)S(1)}, bf16[1040,128]{1,0:T(8,128)(2,1)S(1)}, u32[]{:S(2)}, u32[]{:S(2)}) collective-permute-start(bf16[1040,128]{1,0:T(8,128)(2,1)S(1)} %get-tuple-element.15.e1.own_strip), channel_id=1, source_target_pairs={{1,2},{2,1},{4,3},{5,6},{6,5},{7,0},{9,10},{10,9},{12,11},{13,14},... | collective-permute-start | bytes 798728 | tf_op jit(solution)/shard_map/ppermute | solution.py:333
  6.8 5.0 %shard_map.38 = (bf16[2,512,1536]{2,1,0:T(8,128)(2,1)S(1)}, bf16[1040,128]{1,0:T(8,128)(2,1)S(1)}) custom-call(bf16[512,1024]{1,0:T(8,128)(2,1)S(1)} %get-tuple-element.16.up, bf16[528,1024]{1,0:T(8,128)(2,1)S(1)} %get-tuple-element.17.dn, bf16[1040,128]{1,0:T(8,128)(2,1)S(1)} %get-tuple-element.15.e1.own_strip, bf16[1024,1536]{1,0:T(8,128)(2,1)} %w_ref.7), custom_call_target="tpu_custom_call" | custom-call | flops 1000 | bytes 1000 | tf_op jit(solution)/shard_map/pallas_call | solution.py:292
  11.8 7.9 %collective-permute-start.3 = (bf16[1040,128]{1,0:T(8,128)(2,1)S(1)}, bf16[1040,128]{1,0:T(8,128)(2,1)S(1)}, u32[]{:S(2)}, u32[]{:S(2)}) collective-permute-start(bf16[1040,128]{1,0:T(8,128)(2,1)S(1)} %get-tuple-element.19.tie), channel_id=1, source_target_pairs={{0,7},{3,4},{8,15},{11,12},{16,23},{19,20},{24,31},{27,28},{32,39}... | collective-permute-start | bytes 798728 | tf_op jit(solution)/shard_map/ppermute | solution.py:344
  19.7 0.0 copy-done
  19.7 0.0 copy-start.1
  19.8 1.9 %collective-permute-start.4 = (bf16[1040,128]{1,0:T(8,128)(2,1)S(1)}, bf16[1040,128]{1,0:T(8,128)(2,1)S(1)}, u32[]{:S(2)}, u32[]{:S(2)}) collective-permute-start(bf16[1040,128]{1,0:T(8,128)(2,1)S(1)} %shard_map.43), channel_id=1, source_target_pairs={{0,1},{1,0},{2,3},{3,2},{4,5},{5,4},{6,7},{7,6},{8,9},{9,8},{10,11... | collective-permute-start | bytes 798728 | tf_op jit(solution)/shard_map/ppermute | solution.py:349
  21.7 0.0 collective-permute-done.1.up
  21.7 0.0 collective-permute-done.2.dn
  21.7 4.7 %shard_map.40 = (bf16[2,3,128,512]{3,2,1,0:T(8,128)(2,1)S(1)}, bf16[2,2,64,1024]{3,2,1,0:T(8,128)(2,1)S(1)}) custom-call(bf16[512,1024]{1,0:T(8,128)(2,1)S(1)} %collective-permute-done.1.up, bf16[528,1024]{1,0:T(8,128)(2,1)S(1)} %collective-permute-done.2.dn, bf16[2,512,1536]{2,1,0:T(8,128)(2,1)S(1)} %get-tuple-element.18.p_early, ...), custom_call_target="tpu_custom_call" | custom-call | flops 1000 | bytes 1000 | tf_op jit(solution)/shard_map/pallas_call | solution.py:292
  26.4 0.0 collective-permute-done.value
  26.4 4.9 %collective-permute-done.3.got_y = bf16[1040,128]{1,0:T(8,128)(2,1)S(1)} collective-permute-done((bf16[1040,128]{1,0:T(8,128)(2,1)S(1)}, bf16[1040,128]{1,0:T(8,128)(2,1)S(1)}, u32[]{:S(2)}, u32[]{:S(2)}) %collective-permute-start.3) | collective-permute-done | bytes 266272 | tf_op jit(solution)/shard_map/ppermute | solution.py:344
  31.3 0.1 shard_map.42.first
  31.4 0.0 collective-permute-done.4.second
  31.4 0.1 shard_map.44
  31.5 0.9 %collective-permute-start.6 = (bf16[1056,128]{1,0:T(8,128)(2,1)S(1)}, bf16[1056,128]{1,0:T(8,128)(2,1)S(1)}, u32[]{:S(2)}, u32[]{:S(2)}) collective-permute-start(bf16[1056,128]{1,0:T(8,128)(2,1)S(1)} %get-tuple-element.23), channel_id=1, source_target_pairs={{0,8},{8,16},{16,24},{24,32},{32,40},{40,48},{48,56},{56,64},{64,7... | collective-permute-start | bytes 811016 | tf_op jit(solution)/shard_map/ppermute | solution.py:310
  32.3 0.0 collective-permute-start.5
  32.3 0.7 %shard_map.45.kvf = bf16[2,2,64,1024]{3,2,1,0:T(8,128)(2,1)S(1)} custom-call(bf16[1040,128]{1,0:T(8,128)(2,1)S(1)} %shard_map.42.first, bf16[1040,128]{1,0:T(8,128)(2,1)S(1)} %collective-permute-done.4.second, bf16[1024,1536]{1,0:T(8,128)(2,1)S(1)} %copy-done, bf16[1024,128]{1,0:T(8,128)(2,1)S(1)} %get-tuple-element.22.tie), custom_call_target="tpu_custom_call" | custom-call | flops 1000 | bytes 1000 | tf_op jit(solution)/shard_map/pallas_call | solution.py:292
  33.1 6.3 %collective-permute-done.5.up = bf16[1024,128]{1,0:T(8,128)(2,1)S(1)} collective-permute-done((bf16[1024,128]{1,0:T(8,128)(2,1)S(1)}, bf16[1024,128]{1,0:T(8,128)(2,1)S(1)}, u32[]{:S(2)}, u32[]{:S(2)}) %collective-permute-start.5) | collective-permute-done | bytes 262176 | tf_op jit(solution)/shard_map/ppermute | solution.py:310
  39.4 0.0 collective-permute-done.6.down
  39.4 2.8 %shard_map.46 = bf16[16,64,512]{2,1,0:T(8,128)(2,1)} custom-call(bf16[1024,128]{1,0:T(8,128)(2,1)S(1)} %collective-permute-done.5.up, bf16[1056,128]{1,0:T(8,128)(2,1)S(1)} %collective-permute-done.6.down, bf16[1040,128]{1,0:T(8,128)(2,1)S(1)} %shard_map.42.first, bf16[1040,128]{1,0:T(8,128)(2,1)S(1)} %collective-permute-done.4.second, ...), custom_call_target="tpu_custom_call" | custom-call | flops 1000 | bytes 1000 | tf_op jit(solution)/shard_map/pallas_call | solution.py:292
  (4 shorter events, 0.1 us)
Async XLA Ops:
  2.4 17.3 %copy-start = (bf16[1024,1536]{1,0:T(8,128)(2,1)S(1)}, bf16[1024,1536]{1,0:T(8,128)(2,1)}, u32[]{:S(2)}) copy-start(bf16[1024,1536]{1,0:T(8,128)(2,1)} %w_ref.7) | copy-start | bytes 9437188
  2.4 19.3 %collective-permute-start.2 = (bf16[528,1024]{1,0:T(8,128)(2,1)S(1)}, bf16[528,1024]{1,0:T(8,128)(2,1)S(1)}, u32[]{:S(2)}, u32[]{:S(2)}) collective-permute-start(bf16[528,1024]{1,0:T(8,128)(2,1)S(1)} %get-tuple-element.17.dn), channel_id=1, source_target_pairs={{0,8},{8,16},{16,24},{24,32},{32,40},{40,48},{48,56},{56,64},{64,7... | collective-permute-start | bytes 3244040 | tf_op jit(solution)/shard_map/ppermute | solution.py:310
  5.5 16.2 %collective-permute-start.1 = (bf16[512,1024]{1,0:T(8,128)(2,1)S(1)}, bf16[512,1024]{1,0:T(8,128)(2,1)S(1)}, u32[]{:S(2)}, u32[]{:S(2)}) collective-permute-start(bf16[512,1024]{1,0:T(8,128)(2,1)S(1)} %get-tuple-element.16.up), channel_id=1, source_target_pairs={{0,120},{8,0},{16,8},{24,16},{32,24},{40,32},{48,40},{56,48},{64,5... | collective-permute-start | bytes 3145736 | tf_op jit(solution)/shard_map/ppermute | solution.py:310
  5.5 20.9 %collective-permute-start = (bf16[1040,128]{1,0:T(8,128)(2,1)S(1)}, bf16[1040,128]{1,0:T(8,128)(2,1)S(1)}, u32[]{:S(2)}, u32[]{:S(2)}) collective-permute-start(bf16[1040,128]{1,0:T(8,128)(2,1)S(1)} %get-tuple-element.15.e1.own_strip), channel_id=1, source_target_pairs={{1,2},{2,1},{4,3},{5,6},{6,5},{7,0},{9,10},{10,9},{12,11},{13,14},... | collective-permute-start | bytes 798728 | tf_op jit(solution)/shard_map/ppermute | solution.py:333
  11.8 19.5 %collective-permute-start.3 = (bf16[1040,128]{1,0:T(8,128)(2,1)S(1)}, bf16[1040,128]{1,0:T(8,128)(2,1)S(1)}, u32[]{:S(2)}, u32[]{:S(2)}) collective-permute-start(bf16[1040,128]{1,0:T(8,128)(2,1)S(1)} %get-tuple-element.19.tie), channel_id=1, source_target_pairs={{0,7},{3,4},{8,15},{11,12},{16,23},{19,20},{24,31},{27,28},{32,39}... | collective-permute-start | bytes 798728 | tf_op jit(solution)/shard_map/ppermute | solution.py:344
  19.7 2.0 %copy-start.1 = (s32[1,4,256]{2,1,0:T(4,128)S(1)}, s32[1,4,256]{2,1,0:T(4,128)}, u32[]{:S(2)}) copy-start(s32[1,4,256]{2,1,0:T(4,128)} %ord_ref.1) | copy-start | bytes 12292
  19.8 11.6 %collective-permute-start.4 = (bf16[1040,128]{1,0:T(8,128)(2,1)S(1)}, bf16[1040,128]{1,0:T(8,128)(2,1)S(1)}, u32[]{:S(2)}, u32[]{:S(2)}) collective-permute-start(bf16[1040,128]{1,0:T(8,128)(2,1)S(1)} %shard_map.43), channel_id=1, source_target_pairs={{0,1},{1,0},{2,3},{3,2},{4,5},{5,4},{6,7},{7,6},{8,9},{9,8},{10,11... | collective-permute-start | bytes 798728 | tf_op jit(solution)/shard_map/ppermute | solution.py:349
  31.5 7.9 %collective-permute-start.6 = (bf16[1056,128]{1,0:T(8,128)(2,1)S(1)}, bf16[1056,128]{1,0:T(8,128)(2,1)S(1)}, u32[]{:S(2)}, u32[]{:S(2)}) collective-permute-start(bf16[1056,128]{1,0:T(8,128)(2,1)S(1)} %get-tuple-element.23), channel_id=1, source_target_pairs={{0,8},{8,16},{16,24},{24,32},{32,40},{40,48},{48,56},{56,64},{64,7... | collective-permute-start | bytes 811016 | tf_op jit(solution)/shard_map/ppermute | solution.py:310
  32.3 7.0 %collective-permute-start.5 = (bf16[1024,128]{1,0:T(8,128)(2,1)S(1)}, bf16[1024,128]{1,0:T(8,128)(2,1)S(1)}, u32[]{:S(2)}, u32[]{:S(2)}) collective-permute-start(bf16[1024,128]{1,0:T(8,128)(2,1)S(1)} %get-tuple-element.22.tie), channel_id=1, source_target_pairs={{0,120},{8,0},{16,8},{24,16},{32,24},{40,32},{48,40},{56,48},{64,5... | collective-permute-start | bytes 786440 | tf_op jit(solution)/shard_map/ppermute | solution.py:310

commit v4 on v3

--- a/solution.py
+++ b/solution.py
@@ -186,7 +186,8 @@
     pl.when(jnp.logical_not(early))(lambda: body(p_late))
 
 
-def inner_kernel(up, dn, p_early, p_late, w_ref, ord_ref, out, kve):
+def inner_kernel(up, dn, p_early, p_late, w_ref, ord_ref, tie, out, kve):
+    del tie
     by_side(lambda p: inner_windows(up, dn, p, w_ref, ord_ref, out, kve), p_early, p_late)
 
 
@@ -213,28 +214,40 @@
     e1[...] = jnp.where(one_of(far), got_y[...], got_x[...])
 
 
-def merge_kernel(first, second, to_up, to_dn):
-    for e, src in enumerate((first, second)):
-        put_tokens(to_up, 128, 64 * e, get_tokens(src, 128, 0, 64))
-        put_tokens(to_dn, 128, 64 * e, get_tokens(src, 128, 64, 64))
-        to_dn[1024 + 16 * e : 1040 + 16 * e, :] = src[1024:1040, :]
-
-
-def strips_kernel(first, second, w_ref, tie, kvf):
+def split_kernel(strip, to_up, to_dn):
+    put_tokens(to_up, 64, 0, get_tokens(strip, 128, 0, 64))
+    put_tokens(to_dn, 64, 0, get_tokens(strip, 128, 64, 64))
+    to_dn[512:528, :] = strip[1024:1040, :]
+
+
+def gather_kernel(e2, got_up, got_dn, z):
+    odd = lax.rem(lax.axis_index("cols"), 2)
+    at = pl.ds(pl.multiple_of(384 + 64 * (1 - odd), 64), 64)
+    put_tokens(z, 256, 0, get_tokens(e2, 128, 0, 128))
+    put_tokens(z, 256, 128, got_dn[at, :])
+    put_tokens(z, 256, 192, got_up[at, :])
+    z[2048:2064, :] = e2[1024:1040, :]
+    ranks = got_dn[512:528, 768:1024].astype(F32)
+    z[2064:2080, :] = jnp.concatenate([ranks[0:8, :128], ranks[8:16, 128:]], axis=0).astype(BF)
+
+
+def strips_kernel(first, second, w_ref, tie, kvf, kvz):
     del tie
-    for e, src in enumerate((first, second)):
-        kv = jnp.dot(get_tokens(src, 128, 0, 128), w_ref[:, INNER:], preferred_element_type=F32).astype(BF)
-        kvf[e, 0] = kv[0:64]
-        kvf[e, 1] = kv[64:128]
-
-
-def edge_kernel(up, down, first, second, kvf, w_ref, own_strip, dn, p_early, p_late, inner, kve, out_hbm, edge, out, sem):
-    ups = [get_tokens(up, 128, 64 * e, 64) for e in range(2)]
-    downs = [get_tokens(down, 128, 64 * e, 64) for e in range(2)]
-    corners = [get_ranks(down[1024 + 16 * e : 1040 + 16 * e, :]) for e in range(2)]
-    besides = [get_ranks(src[1024:1040, :]) for src in (first, second)]
-    diags = jnp.concatenate(downs + ups, axis=0)
+    tokens = jnp.concatenate([get_tokens(first, 128, 0, 128), get_tokens(second, 256, 0, 256)], axis=0)
+    kv = jnp.dot(tokens, w_ref[:, INNER:], preferred_element_type=F32).astype(BF)
+    for n in range(2):
+        for e in range(2):
+            kvf[e, n] = kv[128 * e + 64 * n : 128 * e + 64 * n + 64]
+        kvz[n] = kv[256 + 64 * n : 320 + 64 * n]
+
+
+def edge_kernel(
+    up, down, first, second, kvf, kvz, w_ref, own_strip, dn, p_early, p_late, inner, kve, out_hbm, edge, out, sem
+):
+    diags = jnp.concatenate([get_tokens(down, 64, 0, 64), get_tokens(up, 64, 0, 64)], axis=0)
     kvd = jnp.dot(diags, w_ref[:, INNER:], preferred_element_type=F32).astype(BF)
+    corners = [get_ranks(down[512:528, :]), get_ranks(second[2064:2080, :])]
+    besides = [get_ranks(first[1024:1040, :]), get_ranks(second[2048:2064, :])]
     mine = get_ranks(own_strip[1024:1040, :])
     copies = [pltpu.make_async_copy(out.at[pl.ds(8 * h, 8)], out_hbm.at[pl.ds(8 * h, 8)], sem.at[h]) for h in range(2)]
     col = lax.axis_index("cols")
@@ -262,7 +275,7 @@
                 own = p[h, pl.ds(pl.multiple_of(384 + 64 * side, 64), 64), :]
                 near = kve[h, side]
                 far = kvf[e, h]
-                cross = kvd[128 * h + 64 * e : 128 * h + 64 * e + 64]
+                cross = kvz[h] if e else kvd[64 * h : 64 * h + 64]
                 keys = jnp.concatenate(
                     [own[:, INNER : 2 * INNER], far[:, :INNER], near[:, :INNER], cross[:, :INNER]], axis=0
                 )
@@ -280,8 +293,7 @@
     by_side(edges, p_early, p_late)
 
 
-STRIP_FLOPS = 1000
-MERGE_FLOPS = 1_000_000_000
+SPLIT_FLOPS = 10000000000
 VMEM = pl.BlockSpec(memory_space=pltpu.VMEM)
 ANY = pl.BlockSpec(memory_space=pl.ANY)
 HBM = pl.BlockSpec(memory_space=pltpu.HBM)
@@ -345,26 +357,31 @@
     p_late = call(
         project_late_kernel, [arr(2, 512, 3 * INNER)], [up, dn, qkv_weight, again], 1_000, anywhere=(3,)
     )
-    e2_again = call(hold_kernel, [arr(1040, 128)], [e2, p_late], 1_000, anywhere=(1,))
-    got_z = lax.ppermute(e2_again, "cols", second)
+    z = call(gather_kernel, [arr(2080, 128)], [e2, got_up, got_dn], 1_000)
+    got_z = lax.ppermute(z, "cols", second)
     inner, kve = call(
         inner_kernel,
         [arr(2, 3, 128, INNER), arr(2, 2, 64, 2 * INNER)],
-        [got_up, got_dn, p_early, p_late, qkv_weight, orders],
-        1_000,
-    )
-    got_x = call(hold_kernel, [arr(1040, 128)], [got_x, kve], MERGE_FLOPS, anywhere=(1,))
-    got_e1 = call(functools.partial(choose_kernel, far), [arr(1040, 128)], [got_x, got_y], MERGE_FLOPS)
-    to_up, to_dn = call(merge_kernel, [arr(1024, 128), arr(1056, 128)], [got_e1, got_z], 1_000)
+        [got_up, got_dn, p_early, p_late, qkv_weight, orders, z],
+        1_000,
+        anywhere=(6,),
+    )
+    got_x = call(hold_kernel, [arr(1040, 128)], [got_x, kve], 1_000, anywhere=(1,))
+    got_e1 = call(functools.partial(choose_kernel, far), [arr(1040, 128)], [got_x, got_y], 1_000)
+    to_up, to_dn = call(split_kernel, [arr(512, 128), arr(528, 128)], [got_e1], SPLIT_FLOPS)
     hop_up = along_rows(to_up, -1)
     hop_dn = along_rows(to_dn, 1)
-    kvf = call(
-        strips_kernel, [arr(2, 2, 64, 2 * INNER)], [got_e1, got_z, qkv_weight, to_up], STRIP_FLOPS, anywhere=(3,)
+    kvf, kvz = call(
+        strips_kernel,
+        [arr(2, 2, 64, 2 * INNER), arr(2, 64, 2 * INNER)],
+        [got_e1, got_z, qkv_weight, to_up],
+        1_000,
+        anywhere=(3,),
     )
     return call(
         edge_kernel,
         [arr(16, 64, INNER)],
-        [hop_up, hop_dn, got_e1, got_z, kvf, qkv_weight, e1, got_dn, p_early, p_late, inner, kve],
+        [hop_up, hop_dn, got_e1, got_z, kvf, kvz, qkv_weight, e1, got_dn, p_early, p_late, inner, kve],
         1_000,
         scratch=[pltpu.VMEM((2, 64, INNER), F32), pltpu.VMEM((16, 64, INNER), BF), pltpu.SemaphoreType.DMA((2,))],
         to_hbm=True,

time: 42.5 us -> 40.8 us (0.960)
  waiting for transfers between devices: 11.1 us -> 8.53 us
  starting transfers between devices: 15 us -> 15.9 us
    ppermute x4, waiting for transfers between devices: 6.29 us -> 2.73 us  [along_rows(): lax.ppermute(value, 'rows', [(i, (i + by) % size) for i in range(size)])]
    ppermute x1, waiting for transfers between devices: 0.01 us -> 3.37 us  [per_device(): got_z = lax.ppermute(z, 'cols', second)]
    ppermute x1, waiting for transfers between devices: 4.85 us -> 2.43 us  [per_device(): got_y = lax.ppermute(again, 'cols', to_late)]
    ppermute x1, starting transfers between devices: 1.92 us -> 2.82 us  [per_device(): got_z = lax.ppermute(z, 'cols', second)]
  transfers between devices with their start and end apart: 7 -> 7, of which waited for: 2 -> 4; matrix products, arithmetic and copies ran while one was open for 0% -> 0% of each run, Pallas kernels for 25% -> 27%
where the time goes in v4:
time: 40.8 us; the launch traced here: 40.6 us
  starting transfers between devices  15.9 us (39%)
  Pallas kernels  15.8 us (39%)
  waiting for transfers between devices  8.53 us (21%)
    pallas_call x10, Pallas kernels, call(): pl.pallas_call(kernel, out_shape=outs[0] if single else tuple(outs), in_s...  15.8 us
    ppermute x1, starting transfers between devices, per_device(): got_y = lax.ppermute(again, 'cols', to_late)  7.85 us
    ppermute x4, starting transfers between devices, along_rows(): lax.ppermute(value, 'rows', [(i, (i + by) % size) for i in range(size)])  3.96 us
    ppermute x1, waiting for transfers between devices, per_device(): got_z = lax.ppermute(z, 'cols', second)  3.37 us
    ppermute x1, starting transfers between devices, per_device(): got_z = lax.ppermute(z, 'cols', second)  2.82 us
    ppermute x4, waiting for transfers between devices, along_rows(): lax.ppermute(value, 'rows', [(i, (i + by) % size) for i in range(size)])  2.73 us
    ppermute x1, waiting for transfers between devices, per_device(): got_y = lax.ppermute(again, 'cols', to_late)  2.43 us
    ppermute x1, starting transfers between devices, per_device(): lax.ppermute(e1, 'cols', [pair for pair in first if pair not in to_late])  1.28 us
  transfers between devices with their start and end apart: 7, of which 4 were waited for; matrix products, arithmetic and copies ran while one was open for 0% of the time, Pallas kernels for 27%

profile of v4, /device:TPU:25, one launch (start us, length us, event | category | flops | bytes accessed | tf_op | source)
XLA Modules:
  0.0 40.6 jit_solution(14406872437702762893)
XLA Ops:
  0.0 2.4 %shard_map.37 = (bf16[512,1024]{1,0:T(8,128)(2,1)S(1)}, bf16[528,1024]{1,0:T(8,128)(2,1)S(1)}, bf16[1040,128]{1,0:T(8,128)(2,1)S(1)}, bf16[1040,128]{1,0:T(8,128)(2,1)S(1)}) custom-call(bf16[16,64,1024]{2,1,0:T(8,128)(2,1)} %x_ref.1, s32[1,4,256]{2,1,0:T(4,128)} %ord_ref.1), custom_call_target="tpu_custom_call" | custom-call | flops 1000 | bytes 1000 | tf_op jit(solution)/shard_map/pallas_call | solution.py:304
  2.4 0.0 copy-start
  2.4 3.1 %collective-permute-start.2 = (bf16[528,1024]{1,0:T(8,128)(2,1)S(1)}, bf16[528,1024]{1,0:T(8,128)(2,1)S(1)}, u32[]{:S(2)}, u32[]{:S(2)}) collective-permute-start(bf16[528,1024]{1,0:T(8,128)(2,1)S(1)} %get-tuple-element.19.dn), channel_id=1, source_target_pairs={{0,8},{8,16},{16,24},{24,32},{32,40},{40,48},{48,56},{56,64},{64,7... | collective-permute-start | bytes 3244040 | tf_op jit(solution)/shard_map/ppermute | solution.py:322
  5.5 0.0 collective-permute-start.1
  5.5 1.3 %collective-permute-start = (bf16[1040,128]{1,0:T(8,128)(2,1)S(1)}, bf16[1040,128]{1,0:T(8,128)(2,1)S(1)}, u32[]{:S(2)}, u32[]{:S(2)}) collective-permute-start(bf16[1040,128]{1,0:T(8,128)(2,1)S(1)} %get-tuple-element.17.e1.own_strip), channel_id=1, source_target_pairs={{1,2},{2,1},{4,3},{5,6},{6,5},{7,0},{9,10},{10,9},{12,11},{13,14},... | collective-permute-start | bytes 798728 | tf_op jit(solution)/shard_map/ppermute | solution.py:345
  6.8 5.0 %shard_map.38 = (bf16[2,512,1536]{2,1,0:T(8,128)(2,1)S(1)}, bf16[1040,128]{1,0:T(8,128)(2,1)S(1)}) custom-call(bf16[512,1024]{1,0:T(8,128)(2,1)S(1)} %get-tuple-element.18.up, bf16[528,1024]{1,0:T(8,128)(2,1)S(1)} %get-tuple-element.19.dn, bf16[1040,128]{1,0:T(8,128)(2,1)S(1)} %get-tuple-element.17.e1.own_strip, bf16[1024,1536]{1,0:T(8,128)(2,1)} %w_ref.7), custom_call_target="tpu_custom_call" | custom-call | flops 1000 | bytes 1000 | tf_op jit(solution)/shard_map/pallas_call | solution.py:304
  11.8 0.0 copy-start.1
  11.8 7.9 %collective-permute-start.3 = (bf16[1040,128]{1,0:T(8,128)(2,1)S(1)}, bf16[1040,128]{1,0:T(8,128)(2,1)S(1)}, u32[]{:S(2)}, u32[]{:S(2)}) collective-permute-start(bf16[1040,128]{1,0:T(8,128)(2,1)S(1)} %get-tuple-element.21.tie), channel_id=1, source_target_pairs={{0,7},{3,4},{8,15},{11,12},{16,23},{19,20},{24,31},{27,28},{32,39}... | collective-permute-start | bytes 798728 | tf_op jit(solution)/shard_map/ppermute | solution.py:356
  19.7 0.0 copy-done
  19.7 1.5 %collective-permute-done.1.got_up.up = bf16[512,1024]{1,0:T(8,128)(2,1)S(1)} collective-permute-done((bf16[512,1024]{1,0:T(8,128)(2,1)S(1)}, bf16[512,1024]{1,0:T(8,128)(2,1)S(1)}, u32[]{:S(2)}, u32[]{:S(2)}) %collective-permute-start.1) | collective-permute-done | bytes 1048608 | tf_op jit(solution)/shard_map/ppermute | solution.py:322
  21.2 0.0 collective-permute-done.2.got_dn.dn
  21.2 0.1 shard_map.40.tie
  21.3 2.8 %collective-permute-start.6 = (bf16[2080,128]{1,0:T(8,128)(2,1)S(1)}, bf16[2080,128]{1,0:T(8,128)(2,1)S(1)}, u32[]{:S(2)}, u32[]{:S(2)}) collective-permute-start(bf16[2080,128]{1,0:T(8,128)(2,1)S(1)} %shard_map.40.tie), channel_id=1, source_target_pairs={{0,1},{1,0},{2,3},{3,2},{4,5},{5,4},{6,7},{7,6},{8,9},{9,8},{10,11... | collective-permute-start | bytes 1597448 | tf_op jit(solution)/shard_map/ppermute | solution.py:361
  24.1 4.7 %shard_map.41 = (bf16[2,3,128,512]{3,2,1,0:T(8,128)(2,1)S(1)}, bf16[2,2,64,1024]{3,2,1,0:T(8,128)(2,1)S(1)}) custom-call(bf16[512,1024]{1,0:T(8,128)(2,1)S(1)} %collective-permute-done.1.got_up.up, bf16[528,1024]{1,0:T(8,128)(2,1)S(1)} %collective-permute-done.2.got_dn.dn, bf16[2,512,1536]{2,1,0:T(8,128)(2,1)S(1)} %get-tuple-element.20.p_early, ...), custom_call_target="tpu_custom_call" | custom-call | flops 1000 | bytes 1000 | tf_op jit(solution)/shard_map/pallas_call | solution.py:304
  28.8 0.0 collective-permute-done.value
  28.9 2.4 %collective-permute-done.3.got_y = bf16[1040,128]{1,0:T(8,128)(2,1)S(1)} collective-permute-done((bf16[1040,128]{1,0:T(8,128)(2,1)S(1)}, bf16[1040,128]{1,0:T(8,128)(2,1)S(1)}, u32[]{:S(2)}, u32[]{:S(2)}) %collective-permute-start.3) | collective-permute-done | bytes 266272 | tf_op jit(solution)/shard_map/ppermute | solution.py:356
  31.3 0.1 shard_map.43.strip.first
  31.4 0.9 %collective-permute-start.5 = (bf16[528,128]{1,0:T(8,128)(2,1)S(1)}, bf16[528,128]{1,0:T(8,128)(2,1)S(1)}, u32[]{:S(2)}, u32[]{:S(2)}) collective-permute-start(bf16[528,128]{1,0:T(8,128)(2,1)S(1)} %get-tuple-element.25), channel_id=1, source_target_pairs={{0,8},{8,16},{16,24},{24,32},{32,40},{40,48},{48,56},{56,64},{64,7... | collective-permute-start | bytes 405512 | tf_op jit(solution)/shard_map/ppermute | solution.py:322
  32.3 0.0 collective-permute-start.4
  32.3 3.4 %collective-permute-done.6.second = bf16[2080,128]{1,0:T(8,128)(2,1)S(1)} collective-permute-done((bf16[2080,128]{1,0:T(8,128)(2,1)S(1)}, bf16[2080,128]{1,0:T(8,128)(2,1)S(1)}, u32[]{:S(2)}, u32[]{:S(2)}) %collective-permute-start.6) | collective-permute-done | bytes 532512 | tf_op jit(solution)/shard_map/ppermute | solution.py:361
  35.7 1.0 %shard_map.45 = (bf16[2,2,64,1024]{3,2,1,0:T(8,128)(2,1)S(1)}, bf16[2,64,1024]{2,1,0:T(8,128)(2,1)S(1)}) custom-call(bf16[1040,128]{1,0:T(8,128)(2,1)S(1)} %shard_map.43.strip.first, bf16[2080,128]{1,0:T(8,128)(2,1)S(1)} %collective-permute-done.6.second, bf16[1024,1536]{1,0:T(8,128)(2,1)S(1)} %copy-done, bf16[512,128]{1,0:T(8,128)(2,1)S(1)} %get-tuple-element.24.tie), custom_call_target="tpu_custom_call" | custom-call | flops 1000 | bytes 1000 | tf_op jit(solution)/shard_map/pallas_call | solution.py:304
  36.7 1.2 %collective-permute-done.4.up = bf16[512,128]{1,0:T(8,128)(2,1)S(1)} collective-permute-done((bf16[512,128]{1,0:T(8,128)(2,1)S(1)}, bf16[512,128]{1,0:T(8,128)(2,1)S(1)}, u32[]{:S(2)}, u32[]{:S(2)}) %collective-permute-start.4) | collective-permute-done | bytes 131104 | tf_op jit(solution)/shard_map/ppermute | solution.py:322
  37.9 0.0 collective-permute-done.5.down
  37.9 2.5 %shard_map.46 = bf16[16,64,512]{2,1,0:T(8,128)(2,1)} custom-call(bf16[512,128]{1,0:T(8,128)(2,1)S(1)} %collective-permute-done.4.up, bf16[528,128]{1,0:T(8,128)(2,1)S(1)} %collective-permute-done.5.down, bf16[1040,128]{1,0:T(8,128)(2,1)S(1)} %shard_map.43.strip.first, bf16[2080,128]{1,0:T(8,128)(2,1)S(1)} %collective-permute-done.6.second, ...), custom_call_target="tpu_custom_call" | custom-call | flops 1000 | bytes 1000 | tf_op jit(solution)/shard_map/pallas_call | solution.py:304
  (4 shorter events, 0.1 us)
Async XLA Ops:
  2.4 17.3 %copy-start = (bf16[1024,1536]{1,0:T(8,128)(2,1)S(1)}, bf16[1024,1536]{1,0:T(8,128)(2,1)}, u32[]{:S(2)}) copy-start(bf16[1024,1536]{1,0:T(8,128)(2,1)} %w_ref.7) | copy-start | bytes 9437188
  2.4 18.8 %collective-permute-start.2 = (bf16[528,1024]{1,0:T(8,128)(2,1)S(1)}, bf16[528,1024]{1,0:T(8,128)(2,1)S(1)}, u32[]{:S(2)}, u32[]{:S(2)}) collective-permute-start(bf16[528,1024]{1,0:T(8,128)(2,1)S(1)} %get-tuple-element.19.dn), channel_id=1, source_target_pairs={{0,8},{8,16},{16,24},{24,32},{32,40},{40,48},{48,56},{56,64},{64,7... | collective-permute-start | bytes 3244040 | tf_op jit(solution)/shard_map/ppermute | solution.py:322
  5.5 15.7 %collective-permute-start.1 = (bf16[512,1024]{1,0:T(8,128)(2,1)S(1)}, bf16[512,1024]{1,0:T(8,128)(2,1)S(1)}, u32[]{:S(2)}, u32[]{:S(2)}) collective-permute-start(bf16[512,1024]{1,0:T(8,128)(2,1)S(1)} %get-tuple-element.18.up), channel_id=1, source_target_pairs={{0,120},{8,0},{16,8},{24,16},{32,24},{40,32},{48,40},{56,48},{64,5... | collective-permute-start | bytes 3145736 | tf_op jit(solution)/shard_map/ppermute | solution.py:322
  5.5 23.4 %collective-permute-start = (bf16[1040,128]{1,0:T(8,128)(2,1)S(1)}, bf16[1040,128]{1,0:T(8,128)(2,1)S(1)}, u32[]{:S(2)}, u32[]{:S(2)}) collective-permute-start(bf16[1040,128]{1,0:T(8,128)(2,1)S(1)} %get-tuple-element.17.e1.own_strip), channel_id=1, source_target_pairs={{1,2},{2,1},{4,3},{5,6},{6,5},{7,0},{9,10},{10,9},{12,11},{13,14},... | collective-permute-start | bytes 798728 | tf_op jit(solution)/shard_map/ppermute | solution.py:345
  11.8 12.3 %copy-start.1 = (s32[1,4,256]{2,1,0:T(4,128)S(1)}, s32[1,4,256]{2,1,0:T(4,128)}, u32[]{:S(2)}) copy-start(s32[1,4,256]{2,1,0:T(4,128)} %ord_ref.1) | copy-start | bytes 12292
  11.8 19.5 %collective-permute-start.3 = (bf16[1040,128]{1,0:T(8,128)(2,1)S(1)}, bf16[1040,128]{1,0:T(8,128)(2,1)S(1)}, u32[]{:S(2)}, u32[]{:S(2)}) collective-permute-start(bf16[1040,128]{1,0:T(8,128)(2,1)S(1)} %get-tuple-element.21.tie), channel_id=1, source_target_pairs={{0,7},{3,4},{8,15},{11,12},{16,23},{19,20},{24,31},{27,28},{32,39}... | collective-permute-start | bytes 798728 | tf_op jit(solution)/shard_map/ppermute | solution.py:356
  21.3 14.4 %collective-permute-start.6 = (bf16[2080,128]{1,0:T(8,128)(2,1)S(1)}, bf16[2080,128]{1,0:T(8,128)(2,1)S(1)}, u32[]{:S(2)}, u32[]{:S(2)}) collective-permute-start(bf16[2080,128]{1,0:T(8,128)(2,1)S(1)} %shard_map.40.tie), channel_id=1, source_target_pairs={{0,1},{1,0},{2,3},{3,2},{4,5},{5,4},{6,7},{7,6},{8,9},{9,8},{10,11... | collective-permute-start | bytes 1597448 | tf_op jit(solution)/shard_map/ppermute | solution.py:361
  31.4 6.5 %collective-permute-start.5 = (bf16[528,128]{1,0:T(8,128)(2,1)S(1)}, bf16[528,128]{1,0:T(8,128)(2,1)S(1)}, u32[]{:S(2)}, u32[]{:S(2)}) collective-permute-start(bf16[528,128]{1,0:T(8,128)(2,1)S(1)} %get-tuple-element.25), channel_id=1, source_target_pairs={{0,8},{8,16},{16,24},{24,32},{32,40},{40,48},{48,56},{56,64},{64,7... | collective-permute-start | bytes 405512 | tf_op jit(solution)/shard_map/ppermute | solution.py:322
  32.3 5.6 %collective-permute-start.4 = (bf16[512,128]{1,0:T(8,128)(2,1)S(1)}, bf16[512,128]{1,0:T(8,128)(2,1)S(1)}, u32[]{:S(2)}, u32[]{:S(2)}) collective-permute-start(bf16[512,128]{1,0:T(8,128)(2,1)S(1)} %get-tuple-element.24.tie), channel_id=1, source_target_pairs={{0,120},{8,0},{16,8},{24,16},{32,24},{40,32},{48,40},{56,48},{64,5... | collective-permute-start | bytes 393224 | tf_op jit(solution)/shard_map/ppermute | solution.py:322

commit v5 on v4

--- a/solution.py
+++ b/solution.py
@@ -231,56 +231,63 @@
     z[2064:2080, :] = jnp.concatenate([ranks[0:8, :128], ranks[8:16, 128:]], axis=0).astype(BF)
 
 
-def strips_kernel(first, second, w_ref, tie, kvf, kvz):
+def edge_window(h, side, ranks, p, near, far, cross):
+    col = lax.axis_index("cols")
+    lane = lax.broadcasted_iota(jnp.int32, (1, 128), 1)
+    is_left = side == 0
+    last_col = jnp.where(is_left, col == 0, col == lax.axis_size("cols") - 1)
+    half_own = ranks[:, 128:] if h == 0 else ranks[:, :128]
+    half_other = ranks[:, :128] if h == 0 else ranks[:, 128:]
+    half_own, half_other = (
+        jnp.where(is_left, jnp.concatenate([x[:, 64:], x[:, :64]], axis=1), x) for x in (half_own, half_other)
+    )
+    far_col = jnp.where((lane >= 64) & last_col, FAR, 0.0)
+    key_ranks = jnp.concatenate([half_own + far_col, half_other + far_col + jnp.where(last_pair(h), FAR, 0.0)], axis=1)
+    allowed = key_ranks <= column_of(half_own, 64)
+    own = p[h, pl.ds(pl.multiple_of(384 + 64 * side, 64), 64), :]
+    keys = jnp.concatenate([own[:, INNER : 2 * INNER], far[:, :INNER], near[:, :INNER], cross[:, :INNER]], axis=0)
+    values = jnp.concatenate([own[:, 2 * INNER :], far[:, INNER:], near[:, INNER:], cross[:, INNER:]], axis=0)
+    return attend(own[:, :INNER], keys, values, allowed)
+
+
+def edge_ranks(h, side, corner, beside, own_strip, dn):
+    mine = get_ranks(own_strip[1024:1040, :])
+    above = dn[512:528, 768:1024].astype(F32)[0:1]
+    return jnp.where(side == 0, corner, above) if h == 0 else jnp.where(side == 0, beside, mine)
+
+
+def strips_kernel(first, second, w_ref, own_strip, dn, p_early, p_late, kve, tie, kvf, done):
     del tie
     tokens = jnp.concatenate([get_tokens(first, 128, 0, 128), get_tokens(second, 256, 0, 256)], axis=0)
     kv = jnp.dot(tokens, w_ref[:, INNER:], preferred_element_type=F32).astype(BF)
-    for n in range(2):
-        for e in range(2):
-            kvf[e, n] = kv[128 * e + 64 * n : 128 * e + 64 * n + 64]
-        kvz[n] = kv[256 + 64 * n : 320 + 64 * n]
+    kvf[0] = kv[0:64]
+    kvf[1] = kv[64:128]
+    side = 1 - lax.rem(lax.axis_index("cols"), 2)
+    corner, beside = get_ranks(second[2064:2080, :]), get_ranks(second[2048:2064, :])
+
+    def windows(p):
+        for h in range(2):
+            ranks = edge_ranks(h, side, corner, beside, own_strip, dn)
+            far, cross = kv[128 + 64 * h : 192 + 64 * h], kv[256 + 64 * h : 320 + 64 * h]
+            done[h] = edge_window(h, side, ranks, p, kve[h, side], far, cross)
+
+    by_side(windows, p_early, p_late)
 
 
 def edge_kernel(
-    up, down, first, second, kvf, kvz, w_ref, own_strip, dn, p_early, p_late, inner, kve, out_hbm, edge, out, sem
+    up, down, first, kvf, done, w_ref, own_strip, dn, p_early, p_late, inner, kve, out_hbm, edge, out, sem
 ):
     diags = jnp.concatenate([get_tokens(down, 64, 0, 64), get_tokens(up, 64, 0, 64)], axis=0)
     kvd = jnp.dot(diags, w_ref[:, INNER:], preferred_element_type=F32).astype(BF)
-    corners = [get_ranks(down[512:528, :]), get_ranks(second[2064:2080, :])]
-    besides = [get_ranks(first[1024:1040, :]), get_ranks(second[2048:2064, :])]
-    mine = get_ranks(own_strip[1024:1040, :])
+    corner, beside = get_ranks(down[512:528, :]), get_ranks(first[1024:1040, :])
     copies = [pltpu.make_async_copy(out.at[pl.ds(8 * h, 8)], out_hbm.at[pl.ds(8 * h, 8)], sem.at[h]) for h in range(2)]
-    col = lax.axis_index("cols")
-    odd = lax.rem(col, 2)
-
-    def edges(p):
-        above = dn[512:528, 768:1024].astype(F32)[0:1]
-        lane = lax.broadcasted_iota(jnp.int32, (1, 128), 1)
+    side = lax.rem(lax.axis_index("cols"), 2)
+
+    def windows(p):
         for h in range(2):
-            for e, (beside, corner) in enumerate(zip(besides, corners)):
-                side = odd if e == 0 else 1 - odd
-                is_left = side == 0
-                last_col = jnp.where(is_left, col == 0, col == lax.axis_size("cols") - 1)
-                ranks = jnp.where(is_left, corner, above) if h == 0 else jnp.where(is_left, beside, mine)
-                half_own = ranks[:, 128:] if h == 0 else ranks[:, :128]
-                half_other = ranks[:, :128] if h == 0 else ranks[:, 128:]
-                half_own, half_other = (
-                    jnp.where(is_left, jnp.concatenate([x[:, 64:], x[:, :64]], axis=1), x) for x in (half_own, half_other)
-                )
-                far_col = jnp.where((lane >= 64) & last_col, FAR, 0.0)
-                key_ranks = jnp.concatenate(
-                    [half_own + far_col, half_other + far_col + jnp.where(last_pair(h), FAR, 0.0)], axis=1
-                )
-                allowed = key_ranks <= column_of(half_own, 64)
-                own = p[h, pl.ds(pl.multiple_of(384 + 64 * side, 64), 64), :]
-                near = kve[h, side]
-                far = kvf[e, h]
-                cross = kvz[h] if e else kvd[64 * h : 64 * h + 64]
-                keys = jnp.concatenate(
-                    [own[:, INNER : 2 * INNER], far[:, :INNER], near[:, :INNER], cross[:, :INNER]], axis=0
-                )
-                values = jnp.concatenate([own[:, 2 * INNER :], far[:, INNER:], near[:, INNER:], cross[:, INNER:]], axis=0)
-                edge[side] = attend(own[:, :INNER], keys, values, allowed)
+            ranks = edge_ranks(h, side, corner, beside, own_strip, dn)
+            edge[side] = edge_window(h, side, ranks, p, kve[h, side], kvf[h], kvd[64 * h : 64 * h + 64])
+            edge[1 - side] = done[h]
             for i in range(HALF):
                 row = [edge[0, 8 * i : 8 * i + 8]]
                 row += [inner[h, j, 16 * i : 16 * i + 16].astype(F32) for j in range(3)]
@@ -290,7 +297,7 @@
         for copy in copies:
             copy.wait()
 
-    by_side(edges, p_early, p_late)
+    by_side(windows, p_early, p_late)
 
 
 SPLIT_FLOPS = 10000000000
@@ -371,17 +378,17 @@
     to_up, to_dn = call(split_kernel, [arr(512, 128), arr(528, 128)], [got_e1], SPLIT_FLOPS)
     hop_up = along_rows(to_up, -1)
     hop_dn = along_rows(to_dn, 1)
-    kvf, kvz = call(
+    kvf, done = call(
         strips_kernel,
-        [arr(2, 2, 64, 2 * INNER), arr(2, 64, 2 * INNER)],
-        [got_e1, got_z, qkv_weight, to_up],
+        [arr(2, 64, 2 * INNER), jax.ShapeDtypeStruct((2, 64, INNER), F32)],
+        [got_e1, got_z, qkv_weight, e1, got_dn, p_early, p_late, kve, to_up],
         1_000,
-        anywhere=(3,),
+        anywhere=(8,),
     )
     return call(
         edge_kernel,
         [arr(16, 64, INNER)],
-        [hop_up, hop_dn, got_e1, got_z, kvf, kvz, qkv_weight, e1, got_dn, p_early, p_late, inner, kve],
+        [hop_up, hop_dn, got_e1, kvf, done, qkv_weight, e1, got_dn, p_early, p_late, inner, kve],
         1_000,
         scratch=[pltpu.VMEM((2, 64, INNER), F32), pltpu.VMEM((16, 64, INNER), BF), pltpu.SemaphoreType.DMA((2,))],
         to_hbm=True,

time: 40.8 us -> 40.4 us (level)
  waiting for transfers between devices: 8.53 us -> 7.78 us
    ppermute x4, waiting for transfers between devices: 2.73 us -> 1.97 us  [along_rows(): lax.ppermute(value, 'rows', [(i, (i + by) % size) for i in range(size)])]
  transfers between devices with their start and end apart: 7 -> 7, of which waited for: 4 -> 4; matrix products, arithmetic and copies ran while one was open for 0% -> 0% of each run, Pallas kernels for 27% -> 29%
where the time goes in v5:
time: 40.4 us; the launch traced here: 40.2 us
  Pallas kernels  16.2 us (40%)
  starting transfers between devices  15.9 us (39%)
  waiting for transfers between devices  7.78 us (19%)
    pallas_call x10, Pallas kernels, call(): pl.pallas_call(kernel, out_shape=outs[0] if single else tuple(outs), in_s...  16.2 us
    ppermute x1, starting transfers between devices, per_device(): got_y = lax.ppermute(again, 'cols', to_late)  7.85 us
    ppermute x4, starting transfers between devices, along_rows(): lax.ppermute(value, 'rows', [(i, (i + by) % size) for i in range(size)])  3.96 us
    ppermute x1, waiting for transfers between devices, per_device(): got_z = lax.ppermute(z, 'cols', second)  3.37 us
    ppermute x1, starting transfers between devices, per_device(): got_z = lax.ppermute(z, 'cols', second)  2.82 us
    ppermute x1, waiting for transfers between devices, per_device(): got_y = lax.ppermute(again, 'cols', to_late)  2.43 us
    ppermute x4, waiting for transfers between devices, along_rows(): lax.ppermute(value, 'rows', [(i, (i + by) % size) for i in range(size)])  1.97 us
    ppermute x1, starting transfers between devices, per_device(): lax.ppermute(e1, 'cols', [pair for pair in first if pair not in to_late])  1.28 us
  transfers between devices with their start and end apart: 7, of which 4 were waited for; matrix products, arithmetic and copies ran while one was open for 0% of the time, Pallas kernels for 29%

profile of v5, /device:TPU:25, one launch (start us, length us, event | category | flops | bytes accessed | tf_op | source)
XLA Modules:
  0.0 40.2 jit_solution(4546719027790246807)
XLA Ops:
  0.0 2.4 %shard_map.37 = (bf16[512,1024]{1,0:T(8,128)(2,1)S(1)}, bf16[528,1024]{1,0:T(8,128)(2,1)S(1)}, bf16[1040,128]{1,0:T(8,128)(2,1)S(1)}, bf16[1040,128]{1,0:T(8,128)(2,1)S(1)}) custom-call(bf16[16,64,1024]{2,1,0:T(8,128)(2,1)} %x_ref.1, s32[1,4,256]{2,1,0:T(4,128)} %ord_ref.1), custom_call_target="tpu_custom_call" | custom-call | flops 1000 | bytes 1000 | tf_op jit(solution)/shard_map/pallas_call | solution.py:311
  2.4 0.0 copy-start
  2.4 3.1 %collective-permute-start.2 = (bf16[528,1024]{1,0:T(8,128)(2,1)S(1)}, bf16[528,1024]{1,0:T(8,128)(2,1)S(1)}, u32[]{:S(2)}, u32[]{:S(2)}) collective-permute-start(bf16[528,1024]{1,0:T(8,128)(2,1)S(1)} %get-tuple-element.19.dn), channel_id=1, source_target_pairs={{0,8},{8,16},{16,24},{24,32},{32,40},{40,48},{48,56},{56,64},{64,7... | collective-permute-start | bytes 3244040 | tf_op jit(solution)/shard_map/ppermute | solution.py:329
  5.5 0.0 collective-permute-start.1
  5.5 1.3 %collective-permute-start = (bf16[1040,128]{1,0:T(8,128)(2,1)S(1)}, bf16[1040,128]{1,0:T(8,128)(2,1)S(1)}, u32[]{:S(2)}, u32[]{:S(2)}) collective-permute-start(bf16[1040,128]{1,0:T(8,128)(2,1)S(1)} %get-tuple-element.17.e1.own_strip), channel_id=1, source_target_pairs={{1,2},{2,1},{4,3},{5,6},{6,5},{7,0},{9,10},{10,9},{12,11},{13,14},... | collective-permute-start | bytes 798728 | tf_op jit(solution)/shard_map/ppermute | solution.py:352
  6.8 5.0 %shard_map.38 = (bf16[2,512,1536]{2,1,0:T(8,128)(2,1)S(1)}, bf16[1040,128]{1,0:T(8,128)(2,1)S(1)}) custom-call(bf16[512,1024]{1,0:T(8,128)(2,1)S(1)} %get-tuple-element.18.up, bf16[528,1024]{1,0:T(8,128)(2,1)S(1)} %get-tuple-element.19.dn, bf16[1040,128]{1,0:T(8,128)(2,1)S(1)} %get-tuple-element.17.e1.own_strip, bf16[1024,1536]{1,0:T(8,128)(2,1)} %w_ref.7), custom_call_target="tpu_custom_call" | custom-call | flops 1000 | bytes 1000 | tf_op jit(solution)/shard_map/pallas_call | solution.py:311
  11.8 0.0 copy-start.1
  11.8 7.9 %collective-permute-start.3 = (bf16[1040,128]{1,0:T(8,128)(2,1)S(1)}, bf16[1040,128]{1,0:T(8,128)(2,1)S(1)}, u32[]{:S(2)}, u32[]{:S(2)}) collective-permute-start(bf16[1040,128]{1,0:T(8,128)(2,1)S(1)} %get-tuple-element.21.tie), channel_id=1, source_target_pairs={{0,7},{3,4},{8,15},{11,12},{16,23},{19,20},{24,31},{27,28},{32,39}... | collective-permute-start | bytes 798728 | tf_op jit(solution)/shard_map/ppermute | solution.py:363
  19.7 0.0 copy-done
  19.7 1.5 %collective-permute-done.1.got_up.up = bf16[512,1024]{1,0:T(8,128)(2,1)S(1)} collective-permute-done((bf16[512,1024]{1,0:T(8,128)(2,1)S(1)}, bf16[512,1024]{1,0:T(8,128)(2,1)S(1)}, u32[]{:S(2)}, u32[]{:S(2)}) %collective-permute-start.1) | collective-permute-done | bytes 1048608 | tf_op jit(solution)/shard_map/ppermute | solution.py:329
  21.2 0.0 collective-permute-done.2.got_dn.dn
  21.2 0.1 shard_map.40.tie
  21.3 2.8 %collective-permute-start.6 = (bf16[2080,128]{1,0:T(8,128)(2,1)S(1)}, bf16[2080,128]{1,0:T(8,128)(2,1)S(1)}, u32[]{:S(2)}, u32[]{:S(2)}) collective-permute-start(bf16[2080,128]{1,0:T(8,128)(2,1)S(1)} %shard_map.40.tie), channel_id=1, source_target_pairs={{0,1},{1,0},{2,3},{3,2},{4,5},{5,4},{6,7},{7,6},{8,9},{9,8},{10,11... | collective-permute-start | bytes 1597448 | tf_op jit(solution)/shard_map/ppermute | solution.py:368
  24.1 4.7 %shard_map.41 = (bf16[2,3,128,512]{3,2,1,0:T(8,128)(2,1)S(1)}, bf16[2,2,64,1024]{3,2,1,0:T(8,128)(2,1)S(1)}) custom-call(bf16[512,1024]{1,0:T(8,128)(2,1)S(1)} %collective-permute-done.1.got_up.up, bf16[528,1024]{1,0:T(8,128)(2,1)S(1)} %collective-permute-done.2.got_dn.dn, bf16[2,512,1536]{2,1,0:T(8,128)(2,1)S(1)} %get-tuple-element.20.p_early, ...), custom_call_target="tpu_custom_call" | custom-call | flops 1000 | bytes 1000 | tf_op jit(solution)/shard_map/pallas_call | solution.py:311
  28.8 0.0 collective-permute-done.value
  28.9 2.4 %collective-permute-done.3.got_y = bf16[1040,128]{1,0:T(8,128)(2,1)S(1)} collective-permute-done((bf16[1040,128]{1,0:T(8,128)(2,1)S(1)}, bf16[1040,128]{1,0:T(8,128)(2,1)S(1)}, u32[]{:S(2)}, u32[]{:S(2)}) %collective-permute-start.3) | collective-permute-done | bytes 266272 | tf_op jit(solution)/shard_map/ppermute | solution.py:363
  31.3 0.1 shard_map.43.strip.first
  31.4 0.9 %collective-permute-start.5 = (bf16[528,128]{1,0:T(8,128)(2,1)S(1)}, bf16[528,128]{1,0:T(8,128)(2,1)S(1)}, u32[]{:S(2)}, u32[]{:S(2)}) collective-permute-start(bf16[528,128]{1,0:T(8,128)(2,1)S(1)} %get-tuple-element.25), channel_id=1, source_target_pairs={{0,8},{8,16},{16,24},{24,32},{32,40},{40,48},{48,56},{56,64},{64,7... | collective-permute-start | bytes 405512 | tf_op jit(solution)/shard_map/ppermute | solution.py:329
  32.3 0.0 collective-permute-start.4
  32.3 3.4 %collective-permute-done.6.second = bf16[2080,128]{1,0:T(8,128)(2,1)S(1)} collective-permute-done((bf16[2080,128]{1,0:T(8,128)(2,1)S(1)}, bf16[2080,128]{1,0:T(8,128)(2,1)S(1)}, u32[]{:S(2)}, u32[]{:S(2)}) %collective-permute-start.6) | collective-permute-done | bytes 532512 | tf_op jit(solution)/shard_map/ppermute | solution.py:368
  35.7 1.7 %shard_map.45 = (bf16[2,64,1024]{2,1,0:T(8,128)(2,1)S(1)}, f32[2,64,512]{2,1,0:T(8,128)S(1)}) custom-call(bf16[1040,128]{1,0:T(8,128)(2,1)S(1)} %shard_map.43.strip.first, bf16[2080,128]{1,0:T(8,128)(2,1)S(1)} %collective-permute-done.6.second, bf16[1024,1536]{1,0:T(8,128)(2,1)S(1)} %copy-done, bf16[1040,128]{1,0:T(8,128)(2,1)S(1)} %get-tuple-element.17.e1.own_strip, ...), custom_call_target="tpu_custom_call" | custom-call | flops 1000 | bytes 1000 | tf_op jit(solution)/shard_map/pallas_call | solution.py:311
  37.4 0.5 %collective-permute-done.4.up = bf16[512,128]{1,0:T(8,128)(2,1)S(1)} collective-permute-done((bf16[512,128]{1,0:T(8,128)(2,1)S(1)}, bf16[512,128]{1,0:T(8,128)(2,1)S(1)}, u32[]{:S(2)}, u32[]{:S(2)}) %collective-permute-start.4) | collective-permute-done | bytes 131104 | tf_op jit(solution)/shard_map/ppermute | solution.py:329
  37.9 0.0 collective-permute-done.5.down
  37.9 2.2 %shard_map.46 = bf16[16,64,512]{2,1,0:T(8,128)(2,1)} custom-call(bf16[512,128]{1,0:T(8,128)(2,1)S(1)} %collective-permute-done.4.up, bf16[528,128]{1,0:T(8,128)(2,1)S(1)} %collective-permute-done.5.down, bf16[1040,128]{1,0:T(8,128)(2,1)S(1)} %shard_map.43.strip.first, bf16[2,64,1024]{2,1,0:T(8,128)(2,1)S(1)} %get-tuple-element.26.kvf, ...), custom_call_target="tpu_custom_call" | custom-call | flops 1000 | bytes 1000 | tf_op jit(solution)/shard_map/pallas_call | solution.py:311
  (4 shorter events, 0.1 us)
Async XLA Ops:
  2.4 17.3 %copy-start = (bf16[1024,1536]{1,0:T(8,128)(2,1)S(1)}, bf16[1024,1536]{1,0:T(8,128)(2,1)}, u32[]{:S(2)}) copy-start(bf16[1024,1536]{1,0:T(8,128)(2,1)} %w_ref.7) | copy-start | bytes 9437188
  2.4 18.8 %collective-permute-start.2 = (bf16[528,1024]{1,0:T(8,128)(2,1)S(1)}, bf16[528,1024]{1,0:T(8,128)(2,1)S(1)}, u32[]{:S(2)}, u32[]{:S(2)}) collective-permute-start(bf16[528,1024]{1,0:T(8,128)(2,1)S(1)} %get-tuple-element.19.dn), channel_id=1, source_target_pairs={{0,8},{8,16},{16,24},{24,32},{32,40},{40,48},{48,56},{56,64},{64,7... | collective-permute-start | bytes 3244040 | tf_op jit(solution)/shard_map/ppermute | solution.py:329
  5.5 15.7 %collective-permute-start.1 = (bf16[512,1024]{1,0:T(8,128)(2,1)S(1)}, bf16[512,1024]{1,0:T(8,128)(2,1)S(1)}, u32[]{:S(2)}, u32[]{:S(2)}) collective-permute-start(bf16[512,1024]{1,0:T(8,128)(2,1)S(1)} %get-tuple-element.18.up), channel_id=1, source_target_pairs={{0,120},{8,0},{16,8},{24,16},{32,24},{40,32},{48,40},{56,48},{64,5... | collective-permute-start | bytes 3145736 | tf_op jit(solution)/shard_map/ppermute | solution.py:329
  5.5 23.3 %collective-permute-start = (bf16[1040,128]{1,0:T(8,128)(2,1)S(1)}, bf16[1040,128]{1,0:T(8,128)(2,1)S(1)}, u32[]{:S(2)}, u32[]{:S(2)}) collective-permute-start(bf16[1040,128]{1,0:T(8,128)(2,1)S(1)} %get-tuple-element.17.e1.own_strip), channel_id=1, source_target_pairs={{1,2},{2,1},{4,3},{5,6},{6,5},{7,0},{9,10},{10,9},{12,11},{13,14},... | collective-permute-start | bytes 798728 | tf_op jit(solution)/shard_map/ppermute | solution.py:352
  11.8 12.3 %copy-start.1 = (s32[1,4,256]{2,1,0:T(4,128)S(1)}, s32[1,4,256]{2,1,0:T(4,128)}, u32[]{:S(2)}) copy-start(s32[1,4,256]{2,1,0:T(4,128)} %ord_ref.1) | copy-start | bytes 12292
  11.8 19.5 %collective-permute-start.3 = (bf16[1040,128]{1,0:T(8,128)(2,1)S(1)}, bf16[1040,128]{1,0:T(8,128)(2,1)S(1)}, u32[]{:S(2)}, u32[]{:S(2)}) collective-permute-start(bf16[1040,128]{1,0:T(8,128)(2,1)S(1)} %get-tuple-element.21.tie), channel_id=1, source_target_pairs={{0,7},{3,4},{8,15},{11,12},{16,23},{19,20},{24,31},{27,28},{32,39}... | collective-permute-start | bytes 798728 | tf_op jit(solution)/shard_map/ppermute | solution.py:363
  21.3 14.4 %collective-permute-start.6 = (bf16[2080,128]{1,0:T(8,128)(2,1)S(1)}, bf16[2080,128]{1,0:T(8,128)(2,1)S(1)}, u32[]{:S(2)}, u32[]{:S(2)}) collective-permute-start(bf16[2080,128]{1,0:T(8,128)(2,1)S(1)} %shard_map.40.tie), channel_id=1, source_target_pairs={{0,1},{1,0},{2,3},{3,2},{4,5},{5,4},{6,7},{7,6},{8,9},{9,8},{10,11... | collective-permute-start | bytes 1597448 | tf_op jit(solution)/shard_map/ppermute | solution.py:368
  31.4 6.5 %collective-permute-start.5 = (bf16[528,128]{1,0:T(8,128)(2,1)S(1)}, bf16[528,128]{1,0:T(8,128)(2,1)S(1)}, u32[]{:S(2)}, u32[]{:S(2)}) collective-permute-start(bf16[528,128]{1,0:T(8,128)(2,1)S(1)} %get-tuple-element.25), channel_id=1, source_target_pairs={{0,8},{8,16},{16,24},{24,32},{32,40},{40,48},{48,56},{56,64},{64,7... | collective-permute-start | bytes 405512 | tf_op jit(solution)/shard_map/ppermute | solution.py:329
  32.3 5.6 %collective-permute-start.4 = (bf16[512,128]{1,0:T(8,128)(2,1)S(1)}, bf16[512,128]{1,0:T(8,128)(2,1)S(1)}, u32[]{:S(2)}, u32[]{:S(2)}) collective-permute-start(bf16[512,128]{1,0:T(8,128)(2,1)S(1)} %get-tuple-element.24.tie), channel_id=1, source_target_pairs={{0,120},{8,0},{16,8},{24,16},{32,24},{40,32},{48,40},{56,48},{64,5... | collective-permute-start | bytes 393224 | tf_op jit(solution)/shard_map/ppermute | solution.py:329

commit v6 on v5

--- a/solution.py
+++ b/solution.py
@@ -210,14 +210,16 @@
     return functools.reduce(jnp.logical_or, [col == c for c in cols])
 
 
-def choose_kernel(far, got_x, got_y, e1):
-    e1[...] = jnp.where(one_of(far), got_y[...], got_x[...])
-
-
-def split_kernel(strip, to_up, to_dn):
-    put_tokens(to_up, 64, 0, get_tokens(strip, 128, 0, 64))
-    put_tokens(to_dn, 64, 0, get_tokens(strip, 128, 64, 64))
-    to_dn[512:528, :] = strip[1024:1040, :]
+def choose_kernel(far, got_x, got_y, e1, to_up, to_dn):
+    from_y = one_of(far)
+    for src, wanted in ((got_x, jnp.logical_not(from_y)), (got_y, from_y)):
+
+        @pl.when(wanted)
+        def _(src=src):
+            e1[...] = src[...]
+            put_tokens(to_up, 64, 0, get_tokens(src, 128, 0, 64))
+            put_tokens(to_dn, 64, 0, get_tokens(src, 128, 64, 64))
+            to_dn[512:528, :] = src[1024:1040, :]
 
 
 def gather_kernel(e2, got_up, got_dn, z):
@@ -374,8 +376,12 @@
         anywhere=(6,),
     )
     got_x = call(hold_kernel, [arr(1040, 128)], [got_x, kve], 1_000, anywhere=(1,))
-    got_e1 = call(functools.partial(choose_kernel, far), [arr(1040, 128)], [got_x, got_y], 1_000)
-    to_up, to_dn = call(split_kernel, [arr(512, 128), arr(528, 128)], [got_e1], SPLIT_FLOPS)
+    got_e1, to_up, to_dn = call(
+        functools.partial(choose_kernel, far),
+        [arr(1040, 128), arr(512, 128), arr(528, 128)],
+        [got_x, got_y],
+        SPLIT_FLOPS,
+    )
     hop_up = along_rows(to_up, -1)
     hop_dn = along_rows(to_dn, 1)
     kvf, done = call(

time: 40.4 us -> 40.4 us (level)
    pallas_call x10 -> x9, Pallas kernels: 16.2 us -> 16.2 us  [call(): pl.pallas_call(kernel, out_shape=outs[0] if single else tuple(outs), in_s...]
where the time goes in v6:
time: 40.4 us; the launch traced here: 40.2 us
  Pallas kernels  16.2 us (40%)
  starting transfers between devices  15.9 us (39%)
  waiting for transfers between devices  7.78 us (19%)
    pallas_call x9, Pallas kernels, call(): pl.pallas_call(kernel, out_shape=outs[0] if single else tuple(outs), in_s...  16.2 us
    ppermute x1, starting transfers between devices, per_device(): got_y = lax.ppermute(again, 'cols', to_late)  7.85 us
    ppermute x4, starting transfers between devices, along_rows(): lax.ppermute(value, 'rows', [(i, (i + by) % size) for i in range(size)])  3.96 us
    ppermute x1, waiting for transfers between devices, per_device(): got_z = lax.ppermute(z, 'cols', second)  3.41 us
    ppermute x1, starting transfers between devices, per_device(): got_z = lax.ppermute(z, 'cols', second)  2.82 us
    ppermute x1, waiting for transfers between devices, per_device(): got_y = lax.ppermute(again, 'cols', to_late)  2.43 us
    ppermute x4, waiting for transfers between devices, along_rows(): lax.ppermute(value, 'rows', [(i, (i + by) % size) for i in range(size)])  1.94 us
    ppermute x1, starting transfers between devices, per_device(): lax.ppermute(e1, 'cols', [pair for pair in first if pair not in to_late])  1.28 us
  transfers between devices with their start and end apart: 7, of which 4 were waited for; matrix products, arithmetic and copies ran while one was open for 0% of the time, Pallas kernels for 29%

profile of v6, /device:TPU:25, one launch (start us, length us, event | category | flops | bytes accessed | tf_op | source)
XLA Modules:
  0.0 40.2 jit_solution(2109145908871239471)
XLA Ops:
  0.0 2.4 %shard_map.37 = (bf16[512,1024]{1,0:T(8,128)(2,1)S(1)}, bf16[528,1024]{1,0:T(8,128)(2,1)S(1)}, bf16[1040,128]{1,0:T(8,128)(2,1)S(1)}, bf16[1040,128]{1,0:T(8,128)(2,1)S(1)}) custom-call(bf16[16,64,1024]{2,1,0:T(8,128)(2,1)} %x_ref.1, s32[1,4,256]{2,1,0:T(4,128)} %ord_ref.1), custom_call_target="tpu_custom_call" | custom-call | flops 1000 | bytes 1000 | tf_op jit(solution)/shard_map/pallas_call | solution.py:313
  2.4 0.0 copy-start
  2.4 3.1 %collective-permute-start.2 = (bf16[528,1024]{1,0:T(8,128)(2,1)S(1)}, bf16[528,1024]{1,0:T(8,128)(2,1)S(1)}, u32[]{:S(2)}, u32[]{:S(2)}) collective-permute-start(bf16[528,1024]{1,0:T(8,128)(2,1)S(1)} %get-tuple-element.20.dn), channel_id=1, source_target_pairs={{0,8},{8,16},{16,24},{24,32},{32,40},{40,48},{48,56},{56,64},{64,7... | collective-permute-start | bytes 3244040 | tf_op jit(solution)/shard_map/ppermute | solution.py:331
  5.5 0.0 collective-permute-start.1
  5.5 1.3 %collective-permute-start = (bf16[1040,128]{1,0:T(8,128)(2,1)S(1)}, bf16[1040,128]{1,0:T(8,128)(2,1)S(1)}, u32[]{:S(2)}, u32[]{:S(2)}) collective-permute-start(bf16[1040,128]{1,0:T(8,128)(2,1)S(1)} %get-tuple-element.18.e1.own_strip), channel_id=1, source_target_pairs={{1,2},{2,1},{4,3},{5,6},{6,5},{7,0},{9,10},{10,9},{12,11},{13,14},... | collective-permute-start | bytes 798728 | tf_op jit(solution)/shard_map/ppermute | solution.py:354
  6.8 5.0 %shard_map.38 = (bf16[2,512,1536]{2,1,0:T(8,128)(2,1)S(1)}, bf16[1040,128]{1,0:T(8,128)(2,1)S(1)}) custom-call(bf16[512,1024]{1,0:T(8,128)(2,1)S(1)} %get-tuple-element.19.up, bf16[528,1024]{1,0:T(8,128)(2,1)S(1)} %get-tuple-element.20.dn, bf16[1040,128]{1,0:T(8,128)(2,1)S(1)} %get-tuple-element.18.e1.own_strip, bf16[1024,1536]{1,0:T(8,128)(2,1)} %w_ref.7), custom_call_target="tpu_custom_call" | custom-call | flops 1000 | bytes 1000 | tf_op jit(solution)/shard_map/pallas_call | solution.py:313
  11.8 0.0 copy-start.1
  11.8 7.9 %collective-permute-start.3 = (bf16[1040,128]{1,0:T(8,128)(2,1)S(1)}, bf16[1040,128]{1,0:T(8,128)(2,1)S(1)}, u32[]{:S(2)}, u32[]{:S(2)}) collective-permute-start(bf16[1040,128]{1,0:T(8,128)(2,1)S(1)} %get-tuple-element.22.tie), channel_id=1, source_target_pairs={{0,7},{3,4},{8,15},{11,12},{16,23},{19,20},{24,31},{27,28},{32,39}... | collective-permute-start | bytes 798728 | tf_op jit(solution)/shard_map/ppermute | solution.py:365
  19.7 0.0 copy-done
  19.7 1.5 %collective-permute-done.1.got_up.up = bf16[512,1024]{1,0:T(8,128)(2,1)S(1)} collective-permute-done((bf16[512,1024]{1,0:T(8,128)(2,1)S(1)}, bf16[512,1024]{1,0:T(8,128)(2,1)S(1)}, u32[]{:S(2)}, u32[]{:S(2)}) %collective-permute-start.1) | collective-permute-done | bytes 1048608 | tf_op jit(solution)/shard_map/ppermute | solution.py:331
  21.2 0.0 collective-permute-done.2.got_dn.dn
  21.2 0.1 shard_map.40.tie
  21.3 2.8 %collective-permute-start.6 = (bf16[2080,128]{1,0:T(8,128)(2,1)S(1)}, bf16[2080,128]{1,0:T(8,128)(2,1)S(1)}, u32[]{:S(2)}, u32[]{:S(2)}) collective-permute-start(bf16[2080,128]{1,0:T(8,128)(2,1)S(1)} %shard_map.40.tie), channel_id=1, source_target_pairs={{0,1},{1,0},{2,3},{3,2},{4,5},{5,4},{6,7},{7,6},{8,9},{9,8},{10,11... | collective-permute-start | bytes 1597448 | tf_op jit(solution)/shard_map/ppermute | solution.py:370
  24.1 4.7 %shard_map.41 = (bf16[2,3,128,512]{3,2,1,0:T(8,128)(2,1)S(1)}, bf16[2,2,64,1024]{3,2,1,0:T(8,128)(2,1)S(1)}) custom-call(bf16[512,1024]{1,0:T(8,128)(2,1)S(1)} %collective-permute-done.1.got_up.up, bf16[528,1024]{1,0:T(8,128)(2,1)S(1)} %collective-permute-done.2.got_dn.dn, bf16[2,512,1536]{2,1,0:T(8,128)(2,1)S(1)} %get-tuple-element.21.p_early, ...), custom_call_target="tpu_custom_call" | custom-call | flops 1000 | bytes 1000 | tf_op jit(solution)/shard_map/pallas_call | solution.py:313
  28.8 0.0 collective-permute-done.value
  28.9 2.4 %collective-permute-done.3.got_y = bf16[1040,128]{1,0:T(8,128)(2,1)S(1)} collective-permute-done((bf16[1040,128]{1,0:T(8,128)(2,1)S(1)}, bf16[1040,128]{1,0:T(8,128)(2,1)S(1)}, u32[]{:S(2)}, u32[]{:S(2)}) %collective-permute-start.3) | collective-permute-done | bytes 266272 | tf_op jit(solution)/shard_map/ppermute | solution.py:365
  31.3 0.1 shard_map.43
  31.4 0.9 %collective-permute-start.5 = (bf16[528,128]{1,0:T(8,128)(2,1)S(1)}, bf16[528,128]{1,0:T(8,128)(2,1)S(1)}, u32[]{:S(2)}, u32[]{:S(2)}) collective-permute-start(bf16[528,128]{1,0:T(8,128)(2,1)S(1)} %get-tuple-element.26), channel_id=1, source_target_pairs={{0,8},{8,16},{16,24},{24,32},{32,40},{40,48},{48,56},{56,64},{64,7... | collective-permute-start | bytes 405512 | tf_op jit(solution)/shard_map/ppermute | solution.py:331
  32.2 0.0 collective-permute-start.4
  32.2 3.4 %collective-permute-done.6.second = bf16[2080,128]{1,0:T(8,128)(2,1)S(1)} collective-permute-done((bf16[2080,128]{1,0:T(8,128)(2,1)S(1)}, bf16[2080,128]{1,0:T(8,128)(2,1)S(1)}, u32[]{:S(2)}, u32[]{:S(2)}) %collective-permute-start.6) | collective-permute-done | bytes 532512 | tf_op jit(solution)/shard_map/ppermute | solution.py:370
  35.7 1.7 %shard_map.44 = (bf16[2,64,1024]{2,1,0:T(8,128)(2,1)S(1)}, f32[2,64,512]{2,1,0:T(8,128)S(1)}) custom-call(bf16[1040,128]{1,0:T(8,128)(2,1)S(1)} %get-tuple-element.27.first, bf16[2080,128]{1,0:T(8,128)(2,1)S(1)} %collective-permute-done.6.second, bf16[1024,1536]{1,0:T(8,128)(2,1)S(1)} %copy-done, bf16[1040,128]{1,0:T(8,128)(2,1)S(1)} %get-tuple-element.18.e1.own_strip, ...), custom_call_target="tpu_custom_call" | custom-call | flops 1000 | bytes 1000 | tf_op jit(solution)/shard_map/pallas_call | solution.py:313
  37.4 0.5 %collective-permute-done.4.up = bf16[512,128]{1,0:T(8,128)(2,1)S(1)} collective-permute-done((bf16[512,128]{1,0:T(8,128)(2,1)S(1)}, bf16[512,128]{1,0:T(8,128)(2,1)S(1)}, u32[]{:S(2)}, u32[]{:S(2)}) %collective-permute-start.4) | collective-permute-done | bytes 131104 | tf_op jit(solution)/shard_map/ppermute | solution.py:331
  37.8 0.0 collective-permute-done.5.down
  37.9 2.2 %shard_map.45 = bf16[16,64,512]{2,1,0:T(8,128)(2,1)} custom-call(bf16[512,128]{1,0:T(8,128)(2,1)S(1)} %collective-permute-done.4.up, bf16[528,128]{1,0:T(8,128)(2,1)S(1)} %collective-permute-done.5.down, bf16[1040,128]{1,0:T(8,128)(2,1)S(1)} %get-tuple-element.27.first, bf16[2,64,1024]{2,1,0:T(8,128)(2,1)S(1)} %get-tuple-element.28.kvf, ...), custom_call_target="tpu_custom_call" | custom-call | flops 1000 | bytes 1000 | tf_op jit(solution)/shard_map/pallas_call | solution.py:313
  (3 shorter events, 0.0 us)
Async XLA Ops:
  2.4 17.3 %copy-start = (bf16[1024,1536]{1,0:T(8,128)(2,1)S(1)}, bf16[1024,1536]{1,0:T(8,128)(2,1)}, u32[]{:S(2)}) copy-start(bf16[1024,1536]{1,0:T(8,128)(2,1)} %w_ref.7) | copy-start | bytes 9437188
  2.4 18.8 %collective-permute-start.2 = (bf16[528,1024]{1,0:T(8,128)(2,1)S(1)}, bf16[528,1024]{1,0:T(8,128)(2,1)S(1)}, u32[]{:S(2)}, u32[]{:S(2)}) collective-permute-start(bf16[528,1024]{1,0:T(8,128)(2,1)S(1)} %get-tuple-element.20.dn), channel_id=1, source_target_pairs={{0,8},{8,16},{16,24},{24,32},{32,40},{40,48},{48,56},{56,64},{64,7... | collective-permute-start | bytes 3244040 | tf_op jit(solution)/shard_map/ppermute | solution.py:331
  5.5 15.7 %collective-permute-start.1 = (bf16[512,1024]{1,0:T(8,128)(2,1)S(1)}, bf16[512,1024]{1,0:T(8,128)(2,1)S(1)}, u32[]{:S(2)}, u32[]{:S(2)}) collective-permute-start(bf16[512,1024]{1,0:T(8,128)(2,1)S(1)} %get-tuple-element.19.up), channel_id=1, source_target_pairs={{0,120},{8,0},{16,8},{24,16},{32,24},{40,32},{48,40},{56,48},{64,5... | collective-permute-start | bytes 3145736 | tf_op jit(solution)/shard_map/ppermute | solution.py:331
  5.5 23.3 %collective-permute-start = (bf16[1040,128]{1,0:T(8,128)(2,1)S(1)}, bf16[1040,128]{1,0:T(8,128)(2,1)S(1)}, u32[]{:S(2)}, u32[]{:S(2)}) collective-permute-start(bf16[1040,128]{1,0:T(8,128)(2,1)S(1)} %get-tuple-element.18.e1.own_strip), channel_id=1, source_target_pairs={{1,2},{2,1},{4,3},{5,6},{6,5},{7,0},{9,10},{10,9},{12,11},{13,14},... | collective-permute-start | bytes 798728 | tf_op jit(solution)/shard_map/ppermute | solution.py:354
  11.8 12.3 %copy-start.1 = (s32[1,4,256]{2,1,0:T(4,128)S(1)}, s32[1,4,256]{2,1,0:T(4,128)}, u32[]{:S(2)}) copy-start(s32[1,4,256]{2,1,0:T(4,128)} %ord_ref.1) | copy-start | bytes 12292
  11.8 19.5 %collective-permute-start.3 = (bf16[1040,128]{1,0:T(8,128)(2,1)S(1)}, bf16[1040,128]{1,0:T(8,128)(2,1)S(1)}, u32[]{:S(2)}, u32[]{:S(2)}) collective-permute-start(bf16[1040,128]{1,0:T(8,128)(2,1)S(1)} %get-tuple-element.22.tie), channel_id=1, source_target_pairs={{0,7},{3,4},{8,15},{11,12},{16,23},{19,20},{24,31},{27,28},{32,39}... | collective-permute-start | bytes 798728 | tf_op jit(solution)/shard_map/ppermute | solution.py:365
  21.3 14.4 %collective-permute-start.6 = (bf16[2080,128]{1,0:T(8,128)(2,1)S(1)}, bf16[2080,128]{1,0:T(8,128)(2,1)S(1)}, u32[]{:S(2)}, u32[]{:S(2)}) collective-permute-start(bf16[2080,128]{1,0:T(8,128)(2,1)S(1)} %shard_map.40.tie), channel_id=1, source_target_pairs={{0,1},{1,0},{2,3},{3,2},{4,5},{5,4},{6,7},{7,6},{8,9},{9,8},{10,11... | collective-permute-start | bytes 1597448 | tf_op jit(solution)/shard_map/ppermute | solution.py:370
  31.4 6.5 %collective-permute-start.5 = (bf16[528,128]{1,0:T(8,128)(2,1)S(1)}, bf16[528,128]{1,0:T(8,128)(2,1)S(1)}, u32[]{:S(2)}, u32[]{:S(2)}) collective-permute-start(bf16[528,128]{1,0:T(8,128)(2,1)S(1)} %get-tuple-element.26), channel_id=1, source_target_pairs={{0,8},{8,16},{16,24},{24,32},{32,40},{40,48},{48,56},{56,64},{64,7... | collective-permute-start | bytes 405512 | tf_op jit(solution)/shard_map/ppermute | solution.py:331
  32.2 5.6 %collective-permute-start.4 = (bf16[512,128]{1,0:T(8,128)(2,1)S(1)}, bf16[512,128]{1,0:T(8,128)(2,1)S(1)}, u32[]{:S(2)}, u32[]{:S(2)}) collective-permute-start(bf16[512,128]{1,0:T(8,128)(2,1)S(1)} %get-tuple-element.25.tie), channel_id=1, source_target_pairs={{0,120},{8,0},{16,8},{24,16},{32,24},{40,32},{48,40},{56,48},{64,5... | collective-permute-start | bytes 393224 | tf_op jit(solution)/shard_map/ppermute | solution.py:331
